TPU v7x, 32 devices: a whole 2x2x4 slice. The times are simulated.
32 devices in a mesh: groups: 2 (over x), ctx: 8 (over z, y), dp: 2 (over core).
Axes of the slice: x: 2, y: 2, z: 4, core: 2. Of those that a mesh axis runs over, the one named last changes fastest.
Arguments:
- inputs: bfloat16 [4, 4096, 256], P(('groups', 'dp'), 'ctx'), parts along dimension 0, may hold values from -6 to 6
- value_weight: bfloat16 [256, 256], replicated, may hold values from -0.375 to 0.375
- gate_weight: bfloat16 [256, 256], replicated, may hold values from -0.375 to 0.375
- output_weight: bfloat16 [256, 256], replicated, may hold values from -0.375 to 0.375
- filters: bfloat16 [4096, 256], P('ctx'), may hold values from -0.09375 to 0.09375
- cotangent: bfloat16 [4, 4096, 256], P(('groups', 'dp'), 'ctx'), parts along dimension 0, may hold values from -6 to 6
Outputs:
- input_grad: bfloat16 [4, 4096, 256], P(('groups', 'dp'), 'ctx'), parts along dimension 0
- proj_grads: float32 [6, 256, 256], P('groups', 'ctx'), parts along dimension 0
- filter_grads: float32 [8192, 256], P(('groups', 'ctx')), parts along dimension 0
There are 2 independent parts, one for each index of `groups`. A program takes and returns all parts, laid end to end along the dimension named above; an argument that names none is the same for every part. Nothing has to cross between parts.
All inputs are finite; a program needn't handle non-finite values.
Results may differ from a plain program's by a relative error of at most 0.0057.
Values may be sent and summed in bfloat16 or wider, within the bound.
A program may use at most 64 MiB of HBM per device.

v0:
```python
import math

import jax
import jax.numpy as jnp
from jax import lax
from jax.sharding import PartitionSpec as P


def phase_table(left, right, modulus, sign):
    product = left[:, None] * right[None, :] % modulus
    return sign * (2.0 * math.pi / modulus) * product.astype(jnp.float32)


def dft_matrix(size, sign):
    counter = jnp.arange(size, dtype=jnp.int32)
    phase = phase_table(counter, counter, size, sign)
    return (jnp.cos(phase), jnp.sin(phase))


def apply_left(matrix, field):
    return jnp.tensordot(matrix, field, axes=(1, 0), precision=lax.Precision.HIGHEST)


def mix_first(cos_table, sin_table, real_part, imag_part):
    new_real = apply_left(cos_table, real_part) - apply_left(sin_table, imag_part)
    new_imag = apply_left(cos_table, imag_part) + apply_left(sin_table, real_part)
    return (new_real, new_imag)


def apply_middle(matrix, field):
    return jnp.einsum("kb,abw->akw", matrix, field, precision=lax.Precision.HIGHEST)


def mix_second(cos_table, sin_table, real_part, imag_part):
    new_real = apply_middle(cos_table, real_part) - apply_middle(sin_table, imag_part)
    new_imag = apply_middle(cos_table, imag_part) + apply_middle(sin_table, real_part)
    return (new_real, new_imag)


def rotate(real_part, imag_part, cos_part, sin_part):
    return (
        real_part * cos_part - imag_part * sin_part,
        real_part * sin_part + imag_part * cos_part,
    )


def local_dft(real_part, imag_part, sign):
    length = real_part.shape[0]
    columns = real_part.shape[1]
    outer = 32
    inner = length // outer
    real_part = real_part.reshape(outer, inner, columns)
    imag_part = imag_part.reshape(outer, inner, columns)
    cos_table, sin_table = dft_matrix(outer, sign)
    real_part, imag_part = mix_first(cos_table, sin_table, real_part, imag_part)
    phase = phase_table(
        jnp.arange(outer, dtype=jnp.int32), jnp.arange(inner, dtype=jnp.int32), length, sign
    )[:, :, None]
    real_part, imag_part = rotate(real_part, imag_part, jnp.cos(phase), jnp.sin(phase))
    cos_table, sin_table = dft_matrix(inner, sign)
    real_part, imag_part = mix_second(cos_table, sin_table, real_part, imag_part)
    real_part = real_part.transpose(1, 0, 2).reshape(length, columns)
    imag_part = imag_part.transpose(1, 0, 2).reshape(length, columns)
    return (real_part, imag_part)


def forward_transform(stacked):
    count = lax.axis_size("ctx")
    place = lax.axis_index("ctx")
    tok_rows = stacked.shape[0]
    total = count * tok_rows
    piece = tok_rows // count
    moved = lax.all_to_all(stacked[None], "ctx", split_axis=1, concat_axis=0, tiled=True)
    real_rows = moved.astype(jnp.float32)
    cos_table, sin_table = dft_matrix(count, -1.0)
    real_part = apply_left(cos_table, real_rows)
    imag_part = apply_left(sin_table, real_rows)
    row_index = place * piece + jnp.arange(piece, dtype=jnp.int32)
    phase = phase_table(jnp.arange(count, dtype=jnp.int32), row_index, total, -1.0)[:, :, None]
    real_part, imag_part = rotate(real_part, imag_part, jnp.cos(phase), jnp.sin(phase))
    real_part, imag_part = (
        lax.all_to_all(real_part, "ctx", split_axis=0, concat_axis=1, tiled=True),
        lax.all_to_all(imag_part, "ctx", split_axis=0, concat_axis=1, tiled=True),
    )
    return local_dft(real_part[0], imag_part[0], -1.0)


def inverse_transform(real_part, imag_part):
    count = lax.axis_size("ctx")
    place = lax.axis_index("ctx")
    tok_rows = real_part.shape[0]
    total = count * tok_rows
    real_part, imag_part = local_dft(real_part, imag_part, 1.0)
    product = place * jnp.arange(tok_rows, dtype=jnp.int32) % total
    phase = (2.0 * math.pi / total * product.astype(jnp.float32))[:, None]
    real_part, imag_part = rotate(real_part, imag_part, jnp.cos(phase), jnp.sin(phase))
    real_part, imag_part = (
        lax.all_to_all(real_part[None], "ctx", split_axis=1, concat_axis=0, tiled=True),
        lax.all_to_all(imag_part[None], "ctx", split_axis=1, concat_axis=0, tiled=True),
    )
    cos_table, sin_table = dft_matrix(count, 1.0)
    rows_part = apply_left(cos_table, real_part) - apply_left(sin_table, imag_part)
    returned = lax.all_to_all(rows_part, "ctx", split_axis=0, concat_axis=1, tiled=True)
    return returned[0] * (1.0 / total)


def contract_rows(left_rows, right_rows):
    return lax.dot_general(
        left_rows, right_rows, (((0,), (0,)), ((), ())), preferred_element_type=jnp.float32
    )


def times_transpose(left_rows, weight):
    return lax.dot_general(
        left_rows, weight, (((1,), (1,)), ((), ())), preferred_element_type=jnp.float32
    )


def local(inputs, value_weight, gate_weight, output_weight, filters, cotangent):
    token_rows = inputs[0]
    upstream = cotangent[0]
    tok_rows = token_rows.shape[0]
    width = token_rows.shape[1]
    value_act = jnp.dot(token_rows, value_weight, preferred_element_type=jnp.float32).astype(
        jnp.bfloat16
    )
    gate_act = jnp.dot(token_rows, gate_weight, preferred_element_type=jnp.float32)
    d_gated = times_transpose(upstream, output_weight)
    d_mixed = (d_gated * gate_act).astype(jnp.bfloat16)
    share = width // lax.axis_size("dp")
    kernel_part = lax.dynamic_slice_in_dim(filters, lax.axis_index("dp") * share, share, 1)
    spec_real, spec_imag = forward_transform(
        jnp.concatenate([value_act, d_mixed, kernel_part], axis=1)
    )
    value_real = spec_real[:, :width]
    value_imag = spec_imag[:, :width]
    grad_real = spec_real[:, width : 2 * width]
    grad_imag = spec_imag[:, width : 2 * width]
    kernel_real = spec_real[:, 2 * width :]
    kernel_imag = spec_imag[:, 2 * width :]
    kernel_real, kernel_imag = (
        lax.all_gather(kernel_real, "dp", axis=1, tiled=True),
        lax.all_gather(kernel_imag, "dp", axis=1, tiled=True),
    )
    mixed_real = value_real * kernel_real - value_imag * kernel_imag
    mixed_imag = value_real * kernel_imag + value_imag * kernel_real
    back_real = grad_real * kernel_real + grad_imag * kernel_imag
    back_imag = grad_imag * kernel_real - grad_real * kernel_imag
    corr_real = grad_real * value_real + grad_imag * value_imag
    corr_imag = grad_imag * value_real - grad_real * value_imag
    grad_scale = 1.0 / math.sqrt(lax.axis_size("dp") * lax.axis_size("ctx") * tok_rows)
    rows_all = inverse_transform(
        jnp.concatenate([mixed_real, back_real, corr_real], axis=1),
        jnp.concatenate([mixed_imag, back_imag, corr_imag], axis=1),
    )
    mixed_act = rows_all[:, :width]
    d_value = rows_all[:, width : 2 * width].astype(jnp.bfloat16)
    filter_terms = rows_all[:, 2 * width :] * grad_scale
    gated = (gate_act * mixed_act).astype(jnp.bfloat16)
    d_gate = (d_gated * mixed_act).astype(jnp.bfloat16)
    input_rows = times_transpose(d_value, value_weight) + times_transpose(d_gate, gate_weight)
    input_grad = input_rows.astype(jnp.bfloat16)[None]
    proj_terms = (
        jnp.stack(
            [
                contract_rows(token_rows, d_value),
                contract_rows(token_rows, d_gate),
                contract_rows(gated, upstream),
            ],
            axis=0,
        )
        * grad_scale
    )
    proj_part = lax.psum_scatter(proj_terms, "ctx", scatter_dimension=1, tiled=True)
    proj_grads, filter_grads = lax.psum((proj_part, filter_terms), "dp")
    return (input_grad, proj_grads, filter_grads)


def solution(mesh):
    return jax.shard_map(
        local,
        mesh=mesh,
        in_specs=(
            P(("groups", "dp"), "ctx", None),
            P(),
            P(),
            P(),
            P("ctx", None),
            P(("groups", "dp"), "ctx", None),
        ),
        out_specs=(
            P(("groups", "dp"), "ctx", None),
            P("groups", "ctx", None),
            P(("groups", "ctx"), None),
        ),
        check_vma=False,
    )
```

profile of v0, /device:TPU:0, one launch (start us, length us, event | category | flops | bytes accessed | tf_op | source)
XLA Modules:
  0.0 413.0 jit_solution(4538042132011072606)
XLA Ops:
  13.6 4.6 %reduce = bf16[512,640]{1,0:T(8,128)(2,1)S(1)} reduce(bf16[512,1,640]{2,1,0:T(2,128)(2,1)S(1)} %bitcast.141, bf16[]{:T(256)} %broadcast.401), dimensions={1}, to_apply=%bitcast.105.reduce_sub_computation | reduce | bytes 1310722
  19.3 7.3 %all-to-all-start = ((bf16[8,2,20480]{2,1,0:T(2,128)(2,1)}), bf16[8,2,20480]{2,1,0:T(2,128)(2,1)S(1)}, u32[]{:S(2)}, u32[]{:S(2)}) async-start(bf16[8,2,20480]{2,1,0:T(2,128)(2,1)} %reshape.329), calls=%async_computation | async-start | bytes 1310720 | tf_op jit(solution)/shard_map/all_to_all | solution.py:73
  26.8 17.1 %all-to-all-done = bf16[8,2,20480]{2,1,0:T(2,128)(2,1)S(1)} async-done(((bf16[8,2,20480]{2,1,0:T(2,128)(2,1)}), bf16[8,2,20480]{2,1,0:T(2,128)(2,1)S(1)}, u32[]{:S(2)}, u32[]{:S(2)}) %all-to-all-start) | async-done | bytes 655392 | tf_op jit(solution)/shard_map/all_to_all | solution.py:73
  47.9 3.6 all-to-all-start.1
  52.9 30.2 %all-to-all-done.1 = f32[8,64,640]{2,1,0:T(8,128)S(1)} async-done(((f32[8,64,640]{2,1,0:T(8,128)}), f32[8,64,640]{2,1,0:T(8,128)S(1)}, u32[]{:S(2)}, u32[]{:S(2)}) %all-to-all-start.1) | async-done | bytes 1310752 | tf_op jit(solution)/shard_map/all_to_all | solution.py:82
  83.1 3.9 all-to-all-start.2
  87.3 2.6 fusion.31
  89.9 28.5 %all-to-all-done.2 = f32[8,64,640]{2,1,0:T(8,128)S(1)} async-done(((f32[8,64,640]{2,1,0:T(8,128)}), f32[8,64,640]{2,1,0:T(8,128)S(1)}, u32[]{:S(2)}, u32[]{:S(2)}) %all-to-all-start.2) | async-done | bytes 1310752 | tf_op jit(solution)/shard_map/all_to_all | solution.py:83
  121.5 1.9 multiply_subtract_fusion.1
  127.1 12.8 %convolution_subtract_fusion.2 = f32[16,32,640]{2,0,1:T(8,128)S(1)} fusion(f32[16,32,640]{2,0,1:T(8,128)S(1)} %fusion.25, f32[32,16,640]{2,0,1:T(8,128)S(1)} %get-tuple-element.28), kind=kOutput, calls=%fused_computation.32 | convolution fusion | flops 63245824 | bytes 3932160 | tf_op jit(solution)/shard_map/kb,abw->akw/dot_general | solution.py:31
  140.3 2.2 all_gather.6
  142.5 1.9 convolution_add_fusion.2
  144.9 2.2 all_gather.7
  147.5 2.3 fusion.19
  149.9 2.3 fusion.15
  152.3 2.4 convolution_subtract_fusion.1
  154.6 2.7 multiply_subtract_fusion
  157.3 2.4 fusion.13
  159.7 2.2 fusion.9
  161.9 2.2 convolution_subtract_fusion
  165.1 2.2 convolution_add_fusion
  168.6 2.8 copy.121
  171.4 4.1 all-to-all-start.4
  175.5 2.8 copy.119
  178.3 34.6 %all-to-all-done.4 = f32[1,512,768]{2,0,1:T(1,128)S(1)} async-done(((f32[1,512,768]{2,0,1:T(1,128)}), f32[1,512,768]{2,0,1:T(1,128)S(1)}, u32[]{:S(2)}, u32[]{:S(2)}) %all-to-all-start.4) | async-done | bytes 1572896 | tf_op jit(solution)/shard_map/all_to_all | solution.py:99
  212.9 3.6 all-to-all-start.3
  216.7 2.2 fusion.2
  218.9 34.8 %all-to-all-done.3 = f32[1,512,768]{2,0,1:T(1,128)S(1)} async-done(((f32[1,512,768]{2,0,1:T(1,128)}), f32[1,512,768]{2,0,1:T(1,128)S(1)}, u32[]{:S(2)}, u32[]{:S(2)}) %all-to-all-start.3) | async-done | bytes 1572896 | tf_op jit(solution)/shard_map/all_to_all | solution.py:98
  253.8 2.2 fusion.6
  256.5 40.6 %all_to_all.63 = f32[8,64,768]{2,1,0:T(8,128)S(1)} all-to-all(f32[8,64,768]{2,1,0:T(8,128)S(1)} %copy.123), channel_id=1, replica_groups=mesh['groups'=2,'ctx'=8,'dp'=2] {'ctx'}, dimensions={0} | all-to-all | bytes 3145728 | tf_op jit(solution)/shard_map/all_to_all | solution.py:103
  305.0 75.9 %all-reduce.5.cloned.1.call-done = f32[3,256,256]{2,0,1:T(4,128)} async-done(((f32[3,256,256]{2,0,1:T(4,128)}), f32[3,256,256]{2,0,1:T(4,128)}) %all-reduce.5.cloned.1.call-update) | async-done | bytes 786448
  383.7 18.9 %all-reduce.7.cloned.1.call-done = (f32[3,32,256]{2,0,1:T(4,128)}, f32[512,256]{1,0:T(8,128)}) async-done(((f32[3,32,256]{2,0,1:T(4,128)}, f32[512,256]{1,0:T(8,128)}), (f32[3,32,256]{2,0,1:T(4,128)}, f32[512,256]{1,0:T(8,128)})) %all-reduce.7.cloned.1.call-update) | async-done | bytes 622608 | tf_op jit(solution)/shard_map/psum | solution.py:175
  (80 shorter events, 37.7 us)
Async XLA Ops:
  7.2 1.1 copy-start
  7.2 3.7 copy-start.5
  7.2 3.7 copy-start.9
  9.5 1.3 copy-start.2
  19.3 24.6 %all-to-all-start = ((bf16[8,2,20480]{2,1,0:T(2,128)(2,1)}), bf16[8,2,20480]{2,1,0:T(2,128)(2,1)S(1)}, u32[]{:S(2)}, u32[]{:S(2)}) async-start(bf16[8,2,20480]{2,1,0:T(2,128)(2,1)} %reshape.329), calls=%async_computation | async-start | bytes 1310720 | tf_op jit(solution)/shard_map/all_to_all | solution.py:73
  47.9 35.2 %all-to-all-start.1 = ((f32[8,64,640]{2,1,0:T(8,128)}), f32[8,64,640]{2,1,0:T(8,128)S(1)}, u32[]{:S(2)}, u32[]{:S(2)}) async-start(f32[8,64,640]{2,1,0:T(8,128)} %copy.97), calls=%async_computation.1 | async-start | bytes 2621440 | tf_op jit(solution)/shard_map/all_to_all | solution.py:82
  83.1 35.2 %all-to-all-start.2 = ((f32[8,64,640]{2,1,0:T(8,128)}), f32[8,64,640]{2,1,0:T(8,128)S(1)}, u32[]{:S(2)}, u32[]{:S(2)}) async-start(f32[8,64,640]{2,1,0:T(8,128)} %copy.99), calls=%async_computation.2 | async-start | bytes 2621440 | tf_op jit(solution)/shard_map/all_to_all | solution.py:83
  118.3 1.6 copy-start.1
  171.4 41.5 %all-to-all-start.4 = ((f32[1,512,768]{2,0,1:T(1,128)}), f32[1,512,768]{2,0,1:T(1,128)S(1)}, u32[]{:S(2)}, u32[]{:S(2)}) async-start(f32[1,512,768]{2,0,1:T(1,128)} %copy.121), calls=%async_computation.4 | async-start | bytes 3145728 | tf_op jit(solution)/shard_map/all_to_all | solution.py:99
  212.9 40.8 %all-to-all-start.3 = ((f32[1,512,768]{2,0,1:T(1,128)}), f32[1,512,768]{2,0,1:T(1,128)S(1)}, u32[]{:S(2)}, u32[]{:S(2)}) async-start(f32[1,512,768]{2,0,1:T(1,128)} %copy.119), calls=%async_computation.3 | async-start | bytes 3145728 | tf_op jit(solution)/shard_map/all_to_all | solution.py:98
  216.5 164.3 %all-reduce.5.cloned.1.call-start = ((), (), s32[]{:S(2)}) async-start(), calls=%async_computation.6 | async-start | bytes 2097152
  298.3 2.3 copy-start.3
  299.3 2.6 copy-start.4
  300.6 1.6 copy-start.6
  302.3 1.4 copy-start.10
  302.3 80.1 %copy-start.7 = (bf16[256,256]{1,0:T(8,128)(2,1)S(1)}, bf16[256,256]{1,0:T(8,128)(2,1)}, u32[]{:S(2)}) copy-start(bf16[256,256]{1,0:T(8,128)(2,1)} %param.7) | copy-start | bytes 393220
  303.6 79.1 %copy-start.8 = (bf16[256,256]{1,0:T(8,128)(2,1)S(1)}, bf16[256,256]{1,0:T(8,128)(2,1)}, u32[]{:S(2)}) copy-start(bf16[256,256]{1,0:T(8,128)(2,1)} %param.8) | copy-start | bytes 393220
  303.7 98.9 %all-reduce.7.cloned.1.call-start = ((), (), s32[]{:S(2)}) async-start(), calls=%async_computation.7 | async-start | bytes 1310720 | tf_op jit(solution)/shard_map/psum | solution.py:175
Sparse Core Ops, SparseCore 0:
  303.8 77.0 all-reduce.4
  383.9 18.5 all-reduce.6
where the time goes:
time: 420 us; the launch traced here: 413 us
  waiting for transfers between devices  240 us (57%)
  matrix products  58.3 us (14%)
  blocking collectives  44.9 us (11%)
  local copies, waits for them, and re-layouts  24.5 us (6%)
  starting transfers between devices  22.6 us (5%)
  between operations  15.4 us (4%)
  other arithmetic  7.2 us (2%)
    unnamed x3, waiting for transfers between devices  75.9 us
    all_to_all x1, blocking collectives, inverse_transform(): lax.all_to_all(rows_part, 'ctx', split_axis=0, concat_axis=1, tiled=True)  40.6 us
    all_to_all x1, waiting for transfers between devices, inverse_transform(): lax.all_to_all(real_part[None], 'ctx', split_axis=1, concat_axis=0, tiled...  34.8 us
    all_to_all x1, waiting for transfers between devices, inverse_transform(): lax.all_to_all(imag_part[None], 'ctx', split_axis=1, concat_axis=0, tiled...  34.6 us
    all_to_all x1, waiting for transfers between devices, forward_transform(): lax.all_to_all(real_part, 'ctx', split_axis=0, concat_axis=1, tiled=True)  30.2 us
    all_to_all x1, waiting for transfers between devices, forward_transform(): lax.all_to_all(imag_part, 'ctx', split_axis=0, concat_axis=1, tiled=True)  28.5 us
    dot_general x8, matrix products, apply_middle(): jnp.einsum('kb,abw->akw', matrix, field, precision=lax.Precision.HIGHEST)  27.4 us
    dot_general x12, matrix products, apply_left(): jnp.tensordot(matrix, field, axes=(1, 0), precision=lax.Precision.HIGHEST)  23.7 us
  transfers between devices with their start and end apart: 7, of which 7 were waited for; matrix products, arithmetic and copies ran while one was open for 3% of the time, Pallas kernels for 0%

commit v1 on v0

v1 whole, which is shorter than its diff:
```python
import functools
import math

import jax
import jax.numpy as jnp
import numpy as np
from jax import lax
from jax.experimental import pallas as pl
from jax.experimental.pallas import tpu as pltpu
from jax.sharding import PartitionSpec as P

LANES = 128
AXES = ("ctx", "dp")


def dft_tables(length):
    outer = length // LANES
    k_outer = np.arange(outer)
    k_inner = np.arange(LANES)
    first = 2.0 * np.pi / outer * (np.outer(k_outer, k_outer) % outer)
    turn = 2.0 * np.pi / length * (np.outer(k_outer, k_inner) % length)
    second = 2.0 * np.pi / LANES * (np.outer(k_inner, k_inner) % LANES)
    cos_first, sin_first = np.cos(first), np.sin(first)
    cos_second, sin_second = np.cos(second), np.sin(second)
    forward_first = np.concatenate([cos_first, -sin_first], axis=0)
    inverse_first = np.concatenate([cos_first, -sin_first], axis=1) / length
    forward_second = np.block([[cos_second, -sin_second], [sin_second, cos_second]])
    inverse_second = np.block([[cos_second, sin_second], [-sin_second, cos_second]])
    as_float = [
        table.astype(np.float32)
        for table in (forward_first, inverse_first, forward_second, inverse_second)
    ]
    cos_turn = np.cos(turn).astype(np.float32)[:, None, :]
    sin_turn = np.sin(turn).astype(np.float32)[:, None, :]
    return as_float + [cos_turn, sin_turn]


def split(value):
    high = value.astype(jnp.bfloat16)
    low = (value - high.astype(jnp.float32)).astype(jnp.bfloat16)
    return high, low


def split_table(table):
    high = table.astype(jnp.bfloat16)
    return high, (table - high.astype(np.float32)).astype(jnp.bfloat16)


def dot(left, right):
    return jnp.dot(left, right, preferred_element_type=jnp.float32)


def contract(left, left_dim, right, right_dim):
    return lax.dot_general(
        left, right, (((left_dim,), (right_dim,)), ((), ())), preferred_element_type=jnp.float32
    )


def exchange_kernel(count, seqs, sent, held, send_sem, recv_sem, own_sem):
    peers = count * seqs
    me = lax.axis_index("ctx") * seqs + lax.axis_index("dp")
    barrier = pltpu.get_barrier_semaphore()

    def place(step):
        peer = lax.rem(me + step, peers)
        return peer, {"ctx": lax.div(peer, seqs), "dp": lax.rem(peer, seqs)}

    def greet(step, carry):
        pl.semaphore_signal(
            barrier, inc=1, device_id=place(step)[1], device_id_type=pl.DeviceIdType.MESH
        )
        return carry

    lax.fori_loop(1, peers, greet, 0)
    own = pltpu.make_async_copy(sent.at[me], held.at[me], own_sem)
    own.start()
    pl.semaphore_wait(barrier, peers - 1)

    def remote(step):
        peer, target = place(step)
        return pltpu.make_async_remote_copy(
            src_ref=sent.at[peer],
            dst_ref=held.at[me],
            send_sem=send_sem.at[step],
            recv_sem=recv_sem.at[step],
            device_id=target,
            device_id_type=pl.DeviceIdType.MESH,
        )

    def launch(step, carry):
        remote(step).start()
        return carry

    def finish(step, carry):
        remote(step).wait()
        return carry

    lax.fori_loop(1, peers, launch, 0)
    own.wait()
    lax.fori_loop(1, peers, finish, 0)


def exchange(blocks, collective_id):
    count, seqs = lax.axis_size("ctx"), lax.axis_size("dp")
    peers, rows, lanes = blocks.shape
    extra = -rows % 16
    if extra:
        blocks = jnp.pad(blocks, ((0, 0), (0, extra), (0, 0)))
    held = pl.pallas_call(
        functools.partial(exchange_kernel, count, seqs),
        out_shape=jax.ShapeDtypeStruct(blocks.shape, blocks.dtype),
        in_specs=[pl.BlockSpec(memory_space=pltpu.VMEM)],
        out_specs=pl.BlockSpec(memory_space=pltpu.VMEM),
        scratch_shapes=[
            pltpu.SemaphoreType.DMA((peers,)),
            pltpu.SemaphoreType.DMA((peers,)),
            pltpu.SemaphoreType.DMA,
        ],
        compiler_params=pltpu.CompilerParams(
            collective_id=collective_id, has_side_effects=True, vmem_limit_bytes=32 * 2**20
        ),
        name="exchange",
    )(blocks)
    return held[:, :rows] if extra else held


def convolve_all(packed, seqs, share):
    outer, columns, _ = packed.shape
    length = outer * LANES
    wide = seqs * share
    tables = dft_tables(length)
    forward_first, inverse_first, forward_second, inverse_second, cos_turn, sin_turn = tables
    high, low = split_table(forward_first)
    flat = packed.reshape(outer, columns * LANES)
    spread = dot(jnp.concatenate([high, low], axis=1), jnp.concatenate([flat, flat], axis=0))
    spread = spread.reshape(2 * outer, columns, LANES)
    real, imag = spread[:outer], spread[outer:]
    both = jnp.concatenate(
        [real * cos_turn + imag * sin_turn, imag * cos_turn - real * sin_turn], axis=2
    ).reshape(outer * columns, 2 * LANES)
    spec = jnp.dot(both, forward_second, precision=lax.Precision.HIGH)
    spec = spec.reshape(outer, columns, 2 * LANES)
    real, imag = spec[:, :, :LANES], spec[:, :, LANES:]
    kernel_real = real[:, 2 * wide :][:, None]
    kernel_imag = imag[:, 2 * wide :][:, None]
    grouped = (outer, seqs, share, LANES)
    value_real = real[:, :wide].reshape(grouped)
    value_imag = imag[:, :wide].reshape(grouped)
    grad_real = real[:, wide : 2 * wide].reshape(grouped)
    grad_imag = imag[:, wide : 2 * wide].reshape(grouped)
    mixed_real = value_real * kernel_real - value_imag * kernel_imag
    mixed_imag = value_real * kernel_imag + value_imag * kernel_real
    back_real = grad_real * kernel_real + grad_imag * kernel_imag
    back_imag = grad_imag * kernel_real - grad_real * kernel_imag
    corr_real = jnp.sum(grad_real * value_real + grad_imag * value_imag, axis=1)
    corr_imag = jnp.sum(grad_imag * value_real - grad_real * value_imag, axis=1)
    narrow = (outer, wide, LANES)
    out_real = jnp.concatenate(
        [mixed_real.reshape(narrow), back_real.reshape(narrow), corr_real], axis=1
    )
    out_imag = jnp.concatenate(
        [mixed_imag.reshape(narrow), back_imag.reshape(narrow), corr_imag], axis=1
    )
    both = jnp.concatenate([out_real, out_imag], axis=2).reshape(outer * columns, 2 * LANES)
    part = jnp.dot(both, inverse_second, precision=lax.Precision.HIGH)
    part = part.reshape(outer, columns, 2 * LANES)
    real, imag = part[:, :, :LANES], part[:, :, LANES:]
    turned = jnp.concatenate(
        [real * cos_turn - imag * sin_turn, imag * cos_turn + real * sin_turn], axis=0
    ).reshape(2 * outer, columns * LANES)
    rows = jnp.dot(inverse_first, turned, precision=lax.Precision.HIGH)
    return rows.reshape(outer, columns, LANES)


def local(inputs, value_weight, gate_weight, output_weight, filters, cotangent):
    token_rows = inputs[0]
    upstream = cotangent[0]
    tok_rows, width = token_rows.shape
    count = lax.axis_size("ctx")
    seqs = lax.axis_size("dp")
    peers = count * seqs
    share = width // peers
    tiles = tok_rows // LANES
    half = tok_rows // seqs
    value_act = contract(value_weight, 0, token_rows, 1).astype(jnp.bfloat16)
    gate_act = contract(gate_weight, 0, token_rows, 1)
    d_gated = contract(output_weight, 1, upstream, 1)
    d_mixed = (d_gated * gate_act).astype(jnp.bfloat16)
    kernel_part = lax.dynamic_slice_in_dim(filters, lax.axis_index("dp") * half, half, 0).T
    sent = jnp.concatenate(
        [
            value_act.reshape(peers, share * tiles, LANES),
            d_mixed.reshape(peers, share * tiles, LANES),
            kernel_part.reshape(peers, share * half // LANES, LANES),
        ],
        axis=1,
    )
    held = exchange(sent, 0)
    cut = share * tiles
    fields = held[:, : 2 * cut].reshape(count, seqs, 2, share, tiles, LANES)
    fields = fields.transpose(0, 4, 2, 1, 3, 5).reshape(count * tiles, 2 * seqs * share, LANES)
    taps = held[:, 2 * cut :].reshape(count, seqs, share, half // LANES, LANES)
    taps = taps.transpose(0, 1, 3, 2, 4).reshape(count * tiles, share, LANES)
    rows = convolve_all(jnp.concatenate([fields, taps], axis=1), seqs, share)
    grad_scale = 1.0 / math.sqrt(seqs * count * tok_rows)
    wide = seqs * share
    fields = rows[:, : 2 * wide].astype(jnp.bfloat16)
    fields = fields.reshape(count, tiles, 2, seqs, share, LANES).transpose(0, 3, 2, 4, 1, 5)
    terms = (rows[:, 2 * wide :] * grad_scale).astype(jnp.bfloat16)
    terms = terms.reshape(count, tiles, share, LANES).transpose(0, 2, 1, 3)
    terms = jnp.broadcast_to(
        terms.reshape(count, 1, share * tiles, LANES), (count, seqs, share * tiles, LANES)
    )
    back = exchange(
        jnp.concatenate(
            [
                fields.reshape(peers, 2 * share * tiles, LANES),
                terms.reshape(peers, share * tiles, LANES),
            ],
            axis=1,
        ),
        1,
    )
    mixed_act = back[:, :cut].reshape(width, tok_rows).astype(jnp.float32)
    d_value = back[:, cut : 2 * cut].reshape(width, tok_rows)
    filter_grads = back[:, 2 * cut :].reshape(width, tok_rows).T.astype(jnp.float32)
    gated = (gate_act * mixed_act).astype(jnp.bfloat16)
    d_gate = (d_gated * mixed_act).astype(jnp.bfloat16)
    input_rows = contract(d_value, 0, value_weight, 1) + contract(d_gate, 0, gate_weight, 1)
    input_grad = input_rows.astype(jnp.bfloat16)[None]
    proj_terms = jnp.stack(
        [
            contract(token_rows, 0, d_value, 1),
            contract(token_rows, 0, d_gate, 1),
            dot(gated, upstream),
        ],
        axis=0,
    )
    proj_terms = (proj_terms * grad_scale).astype(jnp.bfloat16)
    cell = width // count
    proj_terms = proj_terms.reshape(3, count, cell, width).transpose(1, 0, 2, 3)
    proj_terms = jnp.broadcast_to(
        proj_terms.reshape(count, 1, 3 * cell, width), (count, seqs, 3 * cell, width)
    )
    proj_held = exchange(proj_terms.reshape(peers, 3 * cell, width), 2)
    proj_grads = jnp.sum(proj_held.astype(jnp.float32), axis=0).reshape(3, cell, width)
    return (input_grad, proj_grads, filter_grads)


def solution(mesh):
    return jax.shard_map(
        local,
        mesh=mesh,
        in_specs=(
            P(("groups", "dp"), "ctx", None),
            P(),
            P(),
            P(),
            P("ctx", None),
            P(("groups", "dp"), "ctx", None),
        ),
        out_specs=(
            P(("groups", "dp"), "ctx", None),
            P("groups", "ctx", None),
            P(("groups", "ctx"), None),
        ),
        check_vma=False,
    )
```

time: 420 us -> 87.5 us (0.21)
  the two profiles are of different devices: /device:TPU:0 before, /device:TPU:13 now
where the time goes in v1:
time: 87.5 us; the launch traced here: 86.9 us
  Pallas kernels  62.9 us (72%)
  matrix products  10.9 us (12%)
  local copies, waits for them, and re-layouts  8.04 us (9%)
  other arithmetic  3.91 us (4%)
  between operations  1.12 us (1%)
    pallas_call x3, Pallas kernels, exchange(): pl.pallas_call(functools.partial(exchange_kernel, count, seqs), out_shape...  62.9 us
    unnamed x32, local copies, waits for them, and re-layouts  4.25 us
    dot_general x7, matrix products, contract(): lax.dot_general(left, right, (((left_dim,), (right_dim,)), ((), ())), pre...  4.18 us
    dot_general x1, matrix products, convolve_all(): part = jnp.dot(both, inverse_second, precision=lax.Precision.HIGH)  2.65 us

profile of v1, /device:TPU:13, one launch (start us, length us, event | category | flops | bytes accessed | tf_op | source)
XLA Modules:
  0.0 86.9 jit_solution(17636061211058028990)
XLA Ops:
  0.7 1.0 %dynamic-slice_bitcast_fusion = bf16[256,256]{0,1:T(8,128)(2,1)S(1)} fusion(bf16[512,256]{1,0:T(8,128)(2,1)} %param.17, s32[]{:T(128)S(6)} %select_n.3), kind=kLoop, calls=%fused_computation.81 | loop fusion | bytes 262148 | tf_op jit(solution)/shard_map/transpose | solution.py:189
  1.8 1.2 %convolution_convert_fusion = bf16[256,512]{1,0:T(8,128)(2,1)S(1)} fusion(bf16[256,256]{1,0:T(8,128)(2,1)} %param.14, bf16[1,512,256]{2,1,0:T(8,128)(2,1)S(1)} %copy-done), kind=kOutput, calls=%fused_computation.42 | convolution fusion | flops 67239936 | bytes 655360 | tf_op jit(solution)/shard_map/dot_general | solution.py:54
  3.2 0.3 fusion.45
  3.5 0.3 multiply_convert_fusion.2
  4.0 19.7 %exchange.3 = bf16[16,160,128]{2,1,0:T(8,128)(2,1)S(1)} custom-call(bf16[16,160,128]{2,1,0:T(8,128)(2,1)S(1)} %pad_maximum_fusion.2.sent), custom_call_target="tpu_custom_call" | custom-call | tf_op jit(solution)/shard_map/exchange/pallas_call | solution.py:109
  23.9 0.5 copy-done.13
  24.4 0.5 fusion.27
  24.9 0.2 copy-done.12
  25.1 0.5 convolution_add_fusion
  25.8 0.2 copy.34
  26.1 0.2 copy.35
  26.3 0.5 copy-done.8
  26.8 0.3 fusion.22
  27.1 0.6 copy-done.6
  27.7 1.3 %fusion.3 = f32[32,80,256]{2,1,0:T(8,128)S(1)} fusion(f32[256,256,1]{1,0,2:T(8,128)S(1)} %copy-done.6, f32[32,80,128]{2,1,0:T(8,128)S(1)} %get-tuple-element.10, f32[32,80,128]{2,1,0:T(8,128)S(1)} %get-tuple-element.9), kind=kOutput, calls=%fused_computation.4 | convolution fusion | flops 1007288320 | bytes 5505024 | tf_op jit(solution)/shard_map/dot_general | solution.py:141
  29.0 1.7 %fusion.32 = (f32[32,32,128]{2,1,0:T(8,128)}, f32[32,32,128]{2,1,0:T(8,128)}, f32[32,32,128]{2,1,0:T(8,128)}, f32[32,32,128]{2,1,0:T(8,128)}, f32[32,32,128]{2,1,0:T(8,128)S(1)}, /*index=5*/f32[32,32,128]{2,1,0:T(8,128)S(1)}) fusion(f32[32,80,256]{2,1,0:T(8,128)S(1)} %fusion.3, f32[32,16,128]{2,1,0:T(8,128)S(1)} %get-tuple-element.14, ...), kind=kLoop, calls=%fused_computation.57 | loop fusion | flops 2359296 | bytes 5767168 | tf_op jit(solution)/shard_map/sub | solution.py:151
  30.9 1.0 %copy-done.5 = f32[32,32,128]{2,1,0:T(8,128)S(1)} copy-done((f32[32,32,128]{2,1,0:T(8,128)S(1)}, f32[32,32,128]{2,1,0:T(8,128)}, u32[]{:S(2)}) %copy-start.5) | copy-done | bytes 524312
  31.8 2.7 %fusion.7 = f32[32,80,256]{2,1,0:T(8,128)S(1)} fusion(f32[256,256,1]{1,0,2:T(8,128)} %constant.44, f32[32,16,128]{2,1,0:T(8,128)S(1)} %reduce_sum.28, f32[32,32,128]{2,1,0:T(8,128)} %get-tuple-element.4, f32[32,32,128]{2,1,0:T(8,128)} %get-tuple-element.6, f32[32,16,128]{2,1,0:T(8,128)S(1)} %reduce_sum.27, f32[32,32,128]{2,1,0:T(8,128)} %get-tuple-element.5, ...), kind=kOutput, calls=%fused_computation.8 | convolution fusion | flops 1009909760 | bytes 5505024 | tf_op jit(solution)/shard_map/dot_general | solution.py:165
  34.5 0.3 multiply_subtract_fusion
  35.0 0.5 copy-done.11
  35.5 1.6 %fusion.19 = f32[4,8,80,128]{3,1,2,0:T(8,128)S(1)} fusion(f32[32,64]{1,0:T(8,128)S(1)} %copy-done.11, f32[8,8,80,128]{3,2,1,0:T(8,128)S(1)} %bitcast.132), kind=kOutput, calls=%fused_computation.22 | convolution fusion | flops 125829120 | bytes 3940352 | tf_op jit(solution)/shard_map/dot_general | solution.py:171
  37.2 0.2 copy.37
  37.6 0.4 copy.28
  38.2 21.7 %exchange.4 = bf16[16,192,128]{2,1,0:T(8,128)(2,1)S(1)} custom-call(bf16[16,192,128]{2,1,0:T(8,128)(2,1)S(1)} %pad_maximum_fusion.1.sent), custom_call_target="tpu_custom_call" | custom-call | tf_op jit(solution)/shard_map/exchange/pallas_call | solution.py:109
  60.1 1.0 %copy.32 = f32[256,512]{0,1:T(8,128)} copy(f32[256,512]{1,0:T(8,128)S(1)} %reshape.149) | data formatting | bytes 1048576 | tf_op jit(solution)/shard_map/convert_element_type | solution.py:226
  61.3 1.0 %fusion.43 = f32[256,256]{0,1:T(8,128)} fusion(bf16[256,512]{1,0:T(8,128)(2,1)S(1)} %reshape.144, bf16[1,512,256]{2,1,0:T(8,128)(2,1)S(1)} %copy-done), kind=kOutput, calls=%fused_computation.74 | convolution fusion | flops 67108864 | bytes 786432 | tf_op jit(solution)/shard_map/dot_general | solution.py:54
  62.3 0.3 fusion.51
  62.8 1.0 %fusion.25 = bf16[1,512,256]{2,1,0:T(8,128)(2,1)} fusion(f32[512,256]{1,0:T(8,128)S(1)} %fusion.51, bf16[256,512]{1,0:T(8,128)(2,1)S(1)} %get-tuple-element.21, bf16[256,256]{1,0:T(8,128)(2,1)S(1)} %copy-done.4), kind=kOutput, calls=%fused_computation.44 | convolution fusion | flops 67371008 | bytes 1179648 | tf_op jit(solution)/shard_map/dot_general | solution.py:54
  63.8 0.2 convolution_bitcast_fusion
  64.1 0.3 fusion.41
  64.5 21.6 %exchange.5 = bf16[16,96,256]{2,1,0:T(8,128)(2,1)S(1)} custom-call(bf16[16,96,256]{2,1,0:T(8,128)(2,1)S(1)} %bitcast.131), custom_call_target="tpu_custom_call" | custom-call | tf_op jit(solution)/shard_map/exchange/pallas_call | solution.py:109
  86.1 0.7 convert_reduce_fusion
  (51 shorter events, 2.5 us)
Async XLA Ops:
  0.6 1.2 %copy-start = (bf16[1,512,256]{2,1,0:T(8,128)(2,1)S(1)}, bf16[1,512,256]{2,1,0:T(8,128)(2,1)}, u32[]{:S(2)}) copy-start(bf16[1,512,256]{2,1,0:T(8,128)(2,1)} %param.13) | copy-start | bytes 786436
  0.6 2.5 %copy-start.4 = (bf16[256,256]{1,0:T(8,128)(2,1)S(1)}, bf16[256,256]{1,0:T(8,128)(2,1)}, u32[]{:S(2)}) copy-start(bf16[256,256]{1,0:T(8,128)(2,1)} %param.15) | copy-start | bytes 393220
  1.6 1.8 %copy-start.1 = (bf16[1,512,256]{2,1,0:T(8,128)(2,1)S(1)}, bf16[1,512,256]{2,1,0:T(8,128)(2,1)}, u32[]{:S(2)}) copy-start(bf16[1,512,256]{2,1,0:T(8,128)(2,1)} %param.18) | copy-start | bytes 786436
  1.6 1.8 %copy-start.7 = (bf16[256,256]{1,0:T(8,128)(2,1)S(1)}, bf16[256,256]{1,0:T(8,128)(2,1)}, u32[]{:S(2)}) copy-start(bf16[256,256]{1,0:T(8,128)(2,1)} %param.16) | copy-start | bytes 393220
  23.7 0.7 copy-start.13
  24.4 0.7 copy-start.12
  26.1 0.7 copy-start.8
  26.1 0.7 copy-start.9
  26.8 0.9 %copy-start.6 = (f32[256,256,1]{1,0,2:T(8,128)S(1)}, f32[256,256,1]{1,0,2:T(8,128)}, u32[]{:S(2)}) copy-start(f32[256,256,1]{1,0,2:T(8,128)} %constant.43) | copy-start | bytes 786436
  30.8 1.0 %copy-start.5 = (f32[32,32,128]{2,1,0:T(8,128)S(1)}, f32[32,32,128]{2,1,0:T(8,128)}, u32[]{:S(2)}) copy-start(f32[32,32,128]{2,1,0:T(8,128)} %get-tuple-element.3) | copy-start | bytes 1572868
  31.8 2.7 %copy-start.10 = (f32[32,128]{1,0:T(8,128)S(1)}, f32[32,128]{1,0:T(8,128)}, u32[]{:S(2)}) copy-start(f32[32,128]{1,0:T(8,128)} %constant.39) | copy-start | bytes 49156
  34.8 0.7 copy-start.11
  60.1 2.1 %copy-start.3 = (bf16[256,256]{1,0:T(8,128)(2,1)S(1)}, bf16[256,256]{1,0:T(8,128)(2,1)}, u32[]{:S(2)}) copy-start(bf16[256,256]{1,0:T(8,128)(2,1)} %param.14) | copy-start | bytes 393220
  62.8 1.5 %copy-start.2 = (f32[256,256]{0,1:T(8,128)S(1)}, f32[256,256]{0,1:T(8,128)}, u32[]{:S(2)}) copy-start(f32[256,256]{0,1:T(8,128)} %fusion.43) | copy-start | bytes 786436

commit v2 on v1

--- a/solution.py
+++ b/solution.py
@@ -122,6 +122,107 @@
         name="exchange",
     )(blocks)
     return held[:, :rows] if extra else held
+
+
+def reduce_kernel(count, proj, terms, sums, all_terms, other, stage, held, send_sem, recv_sem, go_sem, come_sem):
+    place = lax.axis_index("ctx")
+    core = lax.axis_index("dp")
+    barrier = pltpu.get_barrier_semaphore()
+
+    def send(source, target, slot):
+        return pltpu.make_async_remote_copy(
+            src_ref=source,
+            dst_ref=target,
+            send_sem=send_sem.at[slot],
+            recv_sem=recv_sem.at[slot],
+            device_id={"dp": 1 - core},
+            device_id_type=pl.DeviceIdType.MESH,
+        )
+
+    def across(step):
+        peer = lax.rem(place + step, count)
+        return pltpu.make_async_remote_copy(
+            src_ref=stage.at[peer],
+            dst_ref=held.at[place],
+            send_sem=go_sem.at[step],
+            recv_sem=come_sem.at[step],
+            device_id={"ctx": peer},
+            device_id_type=pl.DeviceIdType.MESH,
+        )
+
+    def greet(step, carry):
+        pl.semaphore_signal(
+            barrier,
+            inc=1,
+            device_id={"ctx": lax.rem(place + step, count)},
+            device_id_type=pl.DeviceIdType.MESH,
+        )
+        return carry
+
+    def launch(step, carry):
+        across(step).start()
+        return carry
+
+    def finish(step, carry):
+        across(step).wait()
+        return carry
+
+    def add(step, total):
+        return total + held[lax.rem(place + step, count)].astype(jnp.float32)
+
+    pl.semaphore_signal(
+        barrier, inc=1, device_id={"dp": 1 - core}, device_id_type=pl.DeviceIdType.MESH
+    )
+    lax.fori_loop(1, count, greet, 0)
+    pl.semaphore_wait(barrier, count)
+    halves = send(proj.at[1 - core], other, 0)
+    halves.start()
+    taps = send(terms, all_terms.at[core], 1)
+    taps.start()
+    all_terms[core] = terms[...]
+    halves.wait()
+    stage[...] = (proj[core].astype(jnp.float32) + other[...].astype(jnp.float32)).astype(
+        jnp.bfloat16
+    )
+    lax.fori_loop(1, count, launch, 0)
+    taps.wait()
+    lax.fori_loop(1, count, finish, 0)
+    sums[core] = lax.fori_loop(1, count, add, stage[place].astype(jnp.float32))
+    total = send(sums.at[core], sums.at[core], 2)
+    total.start()
+    total.wait()
+
+
+def reduce_and_join(proj, terms, collective_id):
+    count = lax.axis_size("ctx")
+    rows = proj.shape[2]
+    extra = -rows % 16
+    if extra:
+        proj = jnp.pad(proj, ((0, 0), (0, 0), (0, extra), (0, 0)))
+    part = proj.shape[1:]
+    sums, all_terms = pl.pallas_call(
+        functools.partial(reduce_kernel, count),
+        out_shape=(
+            jax.ShapeDtypeStruct((2,) + part[1:], jnp.float32),
+            jax.ShapeDtypeStruct((2,) + terms.shape, terms.dtype),
+        ),
+        in_specs=[pl.BlockSpec(memory_space=pltpu.VMEM)] * 2,
+        out_specs=(pl.BlockSpec(memory_space=pltpu.VMEM),) * 2,
+        scratch_shapes=[
+            pltpu.VMEM(part, jnp.bfloat16),
+            pltpu.VMEM(part, jnp.bfloat16),
+            pltpu.VMEM(part, jnp.bfloat16),
+            pltpu.SemaphoreType.DMA((3,)),
+            pltpu.SemaphoreType.DMA((3,)),
+            pltpu.SemaphoreType.DMA((count,)),
+            pltpu.SemaphoreType.DMA((count,)),
+        ],
+        compiler_params=pltpu.CompilerParams(
+            collective_id=collective_id, has_side_effects=True, vmem_limit_bytes=32 * 2**20
+        ),
+        name="reduce_and_join",
+    )(proj, terms)
+    return sums[:, :rows], all_terms
 
 
 def convolve_all(packed, seqs, share):
@@ -207,15 +308,13 @@
     fields = rows[:, : 2 * wide].astype(jnp.bfloat16)
     fields = fields.reshape(count, tiles, 2, seqs, share, LANES).transpose(0, 3, 2, 4, 1, 5)
     terms = (rows[:, 2 * wide :] * grad_scale).astype(jnp.bfloat16)
-    terms = terms.reshape(count, tiles, share, LANES).transpose(0, 2, 1, 3)
-    terms = jnp.broadcast_to(
-        terms.reshape(count, 1, share * tiles, LANES), (count, seqs, share * tiles, LANES)
-    )
+    near = tiles // seqs
+    terms = terms.reshape(count, seqs, near, share, LANES).transpose(0, 1, 3, 2, 4)
     back = exchange(
         jnp.concatenate(
             [
                 fields.reshape(peers, 2 * share * tiles, LANES),
-                terms.reshape(peers, share * tiles, LANES),
+                terms.reshape(peers, share * near, LANES),
             ],
             axis=1,
         ),
@@ -223,7 +322,6 @@
     )
     mixed_act = back[:, :cut].reshape(width, tok_rows).astype(jnp.float32)
     d_value = back[:, cut : 2 * cut].reshape(width, tok_rows)
-    filter_grads = back[:, 2 * cut :].reshape(width, tok_rows).T.astype(jnp.float32)
     gated = (gate_act * mixed_act).astype(jnp.bfloat16)
     d_gate = (d_gated * mixed_act).astype(jnp.bfloat16)
     input_rows = contract(d_value, 0, value_weight, 1) + contract(d_gate, 0, gate_weight, 1)
@@ -238,12 +336,18 @@
     )
     proj_terms = (proj_terms * grad_scale).astype(jnp.bfloat16)
     cell = width // count
-    proj_terms = proj_terms.reshape(3, count, cell, width).transpose(1, 0, 2, 3)
-    proj_terms = jnp.broadcast_to(
-        proj_terms.reshape(count, 1, 3 * cell, width), (count, seqs, 3 * cell, width)
-    )
-    proj_held = exchange(proj_terms.reshape(peers, 3 * cell, width), 2)
-    proj_grads = jnp.sum(proj_held.astype(jnp.float32), axis=0).reshape(3, cell, width)
+    part = cell // seqs
+    pack = width // LANES
+    proj_terms = proj_terms.reshape(3, count, seqs, part, width).transpose(2, 1, 0, 3, 4)
+    proj_sums, all_terms = reduce_and_join(
+        proj_terms.reshape(seqs, count, 3 * part * pack, LANES),
+        back[:, 2 * cut :].reshape(width * near, LANES),
+        2,
+    )
+    proj_grads = proj_sums.reshape(seqs, 3, part, width).transpose(1, 0, 2, 3)
+    proj_grads = proj_grads.reshape(3, cell, width)
+    filter_grads = all_terms.reshape(seqs, width, half).transpose(0, 2, 1)
+    filter_grads = filter_grads.reshape(tok_rows, width).astype(jnp.float32)
     return (input_grad, proj_grads, filter_grads)
 
 

time: 87.5 us -> 74.7 us (0.85)
  the two profiles are of different devices: /device:TPU:13 before, /device:TPU:0 now
where the time goes in v2:
time: 74.7 us; the launch traced here: 74.1 us
  Pallas kernels  50.7 us (68%)
  matrix products  10.2 us (14%)
  local copies, waits for them, and re-layouts  8.94 us (12%)
  other arithmetic  3.11 us (4%)
  between operations  1.1 us (1%)
    pallas_call x2, Pallas kernels, exchange(): pl.pallas_call(functools.partial(exchange_kernel, count, seqs), out_shape...  36.4 us
    pallas_call x1, Pallas kernels, reduce_and_join(): pl.pallas_call(functools.partial(reduce_kernel, count), out_shape=(jax.Sh...  14.3 us
    unnamed x30, local copies, waits for them, and re-layouts  4.45 us
    dot_general x7, matrix products, contract(): lax.dot_general(left, right, (((left_dim,), (right_dim,)), ((), ())), pre...  3.49 us
    dot_general x1, matrix products, convolve_all(): part = jnp.dot(both, inverse_second, precision=lax.Precision.HIGH)  2.68 us
    sub x1, other arithmetic, convolve_all(): mixed_real = value_real * kernel_real - value_imag * kernel_imag  1.71 us
    dot_general x1, matrix products, convolve_all(): rows = jnp.dot(inverse_first, turned, precision=lax.Precision.HIGH)  1.62 us

profile of v2, /device:TPU:0, one launch (start us, length us, event | category | flops | bytes accessed | tf_op | source)
XLA Modules:
  0.0 74.1 jit_solution(5864294516062955477)
XLA Ops:
  0.7 1.0 %dynamic-slice_bitcast_fusion = bf16[256,256]{0,1:T(8,128)(2,1)S(1)} fusion(bf16[512,256]{1,0:T(8,128)(2,1)} %param.17, s32[]{:T(128)S(6)} %select_n.3), kind=kLoop, calls=%fused_computation.79 | loop fusion | bytes 262148 | tf_op jit(solution)/shard_map/transpose | solution.py:290
  1.8 1.2 %convolution_convert_fusion = bf16[256,512]{1,0:T(8,128)(2,1)S(1)} fusion(bf16[256,256]{1,0:T(8,128)(2,1)} %param.14, bf16[1,512,256]{2,1,0:T(8,128)(2,1)S(1)} %copy-done), kind=kOutput, calls=%fused_computation.41 | convolution fusion | flops 67239936 | bytes 655360 | tf_op jit(solution)/shard_map/dot_general | solution.py:54
  3.2 0.3 fusion.45
  3.5 0.3 multiply_convert_fusion.2
  4.0 17.5 %exchange.2 = bf16[16,160,128]{2,1,0:T(8,128)(2,1)S(1)} custom-call(bf16[16,160,128]{2,1,0:T(8,128)(2,1)S(1)} %pad_maximum_fusion.1.sent), custom_call_target="tpu_custom_call" | custom-call | tf_op jit(solution)/shard_map/exchange/pallas_call | solution.py:109
  21.8 0.5 copy-done.12
  22.3 0.5 fusion.27
  22.7 0.2 copy-done.11
  23.0 0.5 convolution_add_fusion
  23.6 0.2 copy.30
  23.9 0.2 copy.31
  24.2 0.5 copy-done.7
  24.6 0.3 fusion.22
  24.9 0.6 copy-done.5
  25.6 1.2 %fusion.3 = f32[32,80,256]{2,1,0:T(8,128)S(1)} fusion(f32[256,256,1]{1,0,2:T(8,128)S(1)} %copy-done.5, f32[32,80,128]{2,1,0:T(8,128)S(1)} %get-tuple-element.14, f32[32,80,128]{2,1,0:T(8,128)S(1)} %get-tuple-element.13), kind=kOutput, calls=%fused_computation.4 | convolution fusion | flops 1007288320 | bytes 5505024 | tf_op jit(solution)/shard_map/dot_general | solution.py:242
  26.9 1.7 %fusion.32 = (f32[32,32,128]{2,1,0:T(8,128)}, f32[32,32,128]{2,1,0:T(8,128)}, f32[32,32,128]{2,1,0:T(8,128)}, f32[32,32,128]{2,1,0:T(8,128)}, f32[32,32,128]{2,1,0:T(8,128)S(1)}, /*index=5*/f32[32,32,128]{2,1,0:T(8,128)S(1)}) fusion(f32[32,80,256]{2,1,0:T(8,128)S(1)} %fusion.3, f32[32,16,128]{2,1,0:T(8,128)S(1)} %get-tuple-element.18, ...), kind=kLoop, calls=%fused_computation.56 | loop fusion | flops 2359296 | bytes 5767168 | tf_op jit(solution)/shard_map/sub | solution.py:252
  28.7 1.0 %copy-done.4 = f32[32,32,128]{2,1,0:T(8,128)S(1)} copy-done((f32[32,32,128]{2,1,0:T(8,128)S(1)}, f32[32,32,128]{2,1,0:T(8,128)}, u32[]{:S(2)}) %copy-start.4) | copy-done | bytes 524312
  29.6 2.7 %fusion.7 = f32[32,80,256]{2,1,0:T(8,128)S(1)} fusion(f32[256,256,1]{1,0,2:T(8,128)} %constant.44, f32[32,16,128]{2,1,0:T(8,128)S(1)} %reduce_sum.19, f32[32,32,128]{2,1,0:T(8,128)} %get-tuple-element.8, f32[32,32,128]{2,1,0:T(8,128)} %get-tuple-element.10, f32[32,16,128]{2,1,0:T(8,128)S(1)} %reduce_sum.18, f32[32,32,128]{2,1,0:T(8,128)} %get-tuple-element.9, ...), kind=kOutput, calls=%fused_computation.8 | convolution fusion | flops 1009909760 | bytes 5505024 | tf_op jit(solution)/shard_map/dot_general | solution.py:266
  32.3 0.3 multiply_subtract_fusion
  32.9 0.5 copy-done.10
  33.4 1.6 %fusion.19 = f32[4,8,80,128]{3,1,2,0:T(8,128)S(1)} fusion(f32[32,64]{1,0:T(8,128)S(1)} %copy-done.10, f32[8,8,80,128]{3,2,1,0:T(8,128)S(1)} %bitcast.137), kind=kOutput, calls=%fused_computation.21 | convolution fusion | flops 125829120 | bytes 3940352 | tf_op jit(solution)/shard_map/dot_general | solution.py:272
  35.0 0.2 copy.33
  35.4 0.4 copy.23
  36.0 18.9 %exchange.3 = bf16[16,160,128]{2,1,0:T(8,128)(2,1)S(1)} custom-call(bf16[16,160,128]{2,1,0:T(8,128)(2,1)S(1)} %pad_maximum_fusion.3.sent), custom_call_target="tpu_custom_call" | custom-call | tf_op jit(solution)/shard_map/exchange/pallas_call | solution.py:109
  55.3 0.2 convolution_bitcast_fusion
  55.7 0.3 fusion.43
  56.2 0.3 fusion.51
  56.5 1.0 %fusion.25 = bf16[1,512,256]{2,1,0:T(8,128)(2,1)} fusion(f32[512,256]{1,0:T(8,128)S(1)} %fusion.51, bf16[256,512]{1,0:T(8,128)(2,1)S(1)} %get-tuple-element.24, bf16[256,256]{1,0:T(8,128)(2,1)S(1)} %copy-done.3), kind=kOutput, calls=%fused_computation.43 | convolution fusion | flops 67371008 | bytes 1179648 | tf_op jit(solution)/shard_map/dot_general | solution.py:54
  57.4 0.3 fusion.41
  58.0 14.3 %reduce_and_join.1 = (f32[2,96,128]{2,1,0:T(8,128)S(1)}, bf16[2,512,128]{2,1,0:T(8,128)(2,1)S(1)}) custom-call(bf16[2,8,96,128]{3,2,1,0:T(8,128)(2,1)S(1)} %reshape.151.proj, bf16[512,128]{1,0:T(8,128)(2,1)S(1)} %bitcast.136), custom_call_target="tpu_custom_call" | custom-call | tf_op jit(solution)/shard_map/reduce_and_join/pallas_call | solution.py:203
  72.4 0.6 copy.26
  73.1 1.0 %copy.27 = f32[2,256,256]{2,1,0:T(8,128)} copy(f32[2,256,256]{1,2,0:T(8,128)S(1)} %bitcast.146) | data formatting | bytes 1048576 | tf_op jit(solution)/shard_map/convert_element_type | solution.py:350
  (49 shorter events, 2.7 us)
Async XLA Ops:
  0.6 1.2 %copy-start = (bf16[1,512,256]{2,1,0:T(8,128)(2,1)S(1)}, bf16[1,512,256]{2,1,0:T(8,128)(2,1)}, u32[]{:S(2)}) copy-start(bf16[1,512,256]{2,1,0:T(8,128)(2,1)} %param.13) | copy-start | bytes 786436
  0.6 2.5 %copy-start.3 = (bf16[256,256]{1,0:T(8,128)(2,1)S(1)}, bf16[256,256]{1,0:T(8,128)(2,1)}, u32[]{:S(2)}) copy-start(bf16[256,256]{1,0:T(8,128)(2,1)} %param.15) | copy-start | bytes 393220
  1.6 1.8 %copy-start.1 = (bf16[1,512,256]{2,1,0:T(8,128)(2,1)S(1)}, bf16[1,512,256]{2,1,0:T(8,128)(2,1)}, u32[]{:S(2)}) copy-start(bf16[1,512,256]{2,1,0:T(8,128)(2,1)} %param.18) | copy-start | bytes 786436
  1.6 1.8 %copy-start.6 = (bf16[256,256]{1,0:T(8,128)(2,1)S(1)}, bf16[256,256]{1,0:T(8,128)(2,1)}, u32[]{:S(2)}) copy-start(bf16[256,256]{1,0:T(8,128)(2,1)} %param.16) | copy-start | bytes 393220
  21.5 0.7 copy-start.12
  22.3 0.7 copy-start.11
  23.9 0.7 copy-start.7
  23.9 0.7 copy-start.8
  24.6 0.9 %copy-start.5 = (f32[256,256,1]{1,0,2:T(8,128)S(1)}, f32[256,256,1]{1,0,2:T(8,128)}, u32[]{:S(2)}) copy-start(f32[256,256,1]{1,0,2:T(8,128)} %constant.43) | copy-start | bytes 786436
  28.6 1.0 %copy-start.4 = (f32[32,32,128]{2,1,0:T(8,128)S(1)}, f32[32,32,128]{2,1,0:T(8,128)}, u32[]{:S(2)}) copy-start(f32[32,32,128]{2,1,0:T(8,128)} %get-tuple-element.7) | copy-start | bytes 1572868
  29.6 2.7 %copy-start.9 = (f32[32,128]{1,0:T(8,128)S(1)}, f32[32,128]{1,0:T(8,128)}, u32[]{:S(2)}) copy-start(f32[32,128]{1,0:T(8,128)} %constant.39) | copy-start | bytes 49156
  32.7 0.7 copy-start.10
  55.3 0.9 %copy-start.2 = (bf16[256,256]{1,0:T(8,128)(2,1)S(1)}, bf16[256,256]{1,0:T(8,128)(2,1)}, u32[]{:S(2)}) copy-start(bf16[256,256]{1,0:T(8,128)(2,1)} %param.14) | copy-start | bytes 393220

commit v3 on v2

--- a/solution.py
+++ b/solution.py
@@ -225,6 +225,58 @@
     return sums[:, :rows], all_terms
 
 
+def stack_table(table):
+    high, low = split_table(table)
+    return jnp.concatenate([high, high, low], axis=0)
+
+
+def spectra_kernel(seqs, share, spread, cos_ref, sin_ref, forward, inverse, turned):
+    outer = spread.shape[0] // 2
+    columns = spread.shape[1]
+    wide = seqs * share
+    chunk = 8
+
+    def times(real, imag, table):
+        both = jnp.concatenate([real, imag], axis=2).reshape(chunk * columns, 2 * LANES)
+        high, low = split(both)
+        out = dot(jnp.concatenate([high, low, high], axis=1), table[...])
+        out = out.reshape(chunk, columns, 2 * LANES)
+        return out[:, :, :LANES], out[:, :, LANES:]
+
+    def step(index, carry):
+        first = pl.multiple_of(index * chunk, chunk)
+        upper, lower = pl.ds(first, chunk), pl.ds(outer + first, chunk)
+        cos_turn, sin_turn = cos_ref[upper], sin_ref[upper]
+        real, imag = spread[upper], spread[lower]
+        real, imag = times(
+            real * cos_turn + imag * sin_turn, imag * cos_turn - real * sin_turn, forward
+        )
+        kernel_real, kernel_imag = real[:, 2 * wide :], imag[:, 2 * wide :]
+        mixed_reals, mixed_imags, back_reals, back_imags = [], [], [], []
+        corr_real, corr_imag = 0.0, 0.0
+        for seq in range(seqs):
+            near = slice(seq * share, (seq + 1) * share)
+            far = slice(wide + seq * share, wide + (seq + 1) * share)
+            value_real, value_imag = real[:, near], imag[:, near]
+            grad_real, grad_imag = real[:, far], imag[:, far]
+            mixed_reals.append(value_real * kernel_real - value_imag * kernel_imag)
+            mixed_imags.append(value_real * kernel_imag + value_imag * kernel_real)
+            back_reals.append(grad_real * kernel_real + grad_imag * kernel_imag)
+            back_imags.append(grad_imag * kernel_real - grad_real * kernel_imag)
+            corr_real = corr_real + grad_real * value_real + grad_imag * value_imag
+            corr_imag = corr_imag + grad_imag * value_real - grad_real * value_imag
+        real, imag = times(
+            jnp.concatenate(mixed_reals + back_reals + [corr_real], axis=1),
+            jnp.concatenate(mixed_imags + back_imags + [corr_imag], axis=1),
+            inverse,
+        )
+        turned[upper] = real * cos_turn - imag * sin_turn
+        turned[lower] = imag * cos_turn + real * sin_turn
+        return carry
+
+    lax.fori_loop(0, outer // chunk, step, 0)
+
+
 def convolve_all(packed, seqs, share):
     outer, columns, _ = packed.shape
     length = outer * LANES
@@ -235,40 +287,15 @@
     flat = packed.reshape(outer, columns * LANES)
     spread = dot(jnp.concatenate([high, low], axis=1), jnp.concatenate([flat, flat], axis=0))
     spread = spread.reshape(2 * outer, columns, LANES)
-    real, imag = spread[:outer], spread[outer:]
-    both = jnp.concatenate(
-        [real * cos_turn + imag * sin_turn, imag * cos_turn - real * sin_turn], axis=2
-    ).reshape(outer * columns, 2 * LANES)
-    spec = jnp.dot(both, forward_second, precision=lax.Precision.HIGH)
-    spec = spec.reshape(outer, columns, 2 * LANES)
-    real, imag = spec[:, :, :LANES], spec[:, :, LANES:]
-    kernel_real = real[:, 2 * wide :][:, None]
-    kernel_imag = imag[:, 2 * wide :][:, None]
-    grouped = (outer, seqs, share, LANES)
-    value_real = real[:, :wide].reshape(grouped)
-    value_imag = imag[:, :wide].reshape(grouped)
-    grad_real = real[:, wide : 2 * wide].reshape(grouped)
-    grad_imag = imag[:, wide : 2 * wide].reshape(grouped)
-    mixed_real = value_real * kernel_real - value_imag * kernel_imag
-    mixed_imag = value_real * kernel_imag + value_imag * kernel_real
-    back_real = grad_real * kernel_real + grad_imag * kernel_imag
-    back_imag = grad_imag * kernel_real - grad_real * kernel_imag
-    corr_real = jnp.sum(grad_real * value_real + grad_imag * value_imag, axis=1)
-    corr_imag = jnp.sum(grad_imag * value_real - grad_real * value_imag, axis=1)
-    narrow = (outer, wide, LANES)
-    out_real = jnp.concatenate(
-        [mixed_real.reshape(narrow), back_real.reshape(narrow), corr_real], axis=1
-    )
-    out_imag = jnp.concatenate(
-        [mixed_imag.reshape(narrow), back_imag.reshape(narrow), corr_imag], axis=1
-    )
-    both = jnp.concatenate([out_real, out_imag], axis=2).reshape(outer * columns, 2 * LANES)
-    part = jnp.dot(both, inverse_second, precision=lax.Precision.HIGH)
-    part = part.reshape(outer, columns, 2 * LANES)
-    real, imag = part[:, :, :LANES], part[:, :, LANES:]
-    turned = jnp.concatenate(
-        [real * cos_turn - imag * sin_turn, imag * cos_turn + real * sin_turn], axis=0
-    ).reshape(2 * outer, columns * LANES)
+    turned = pl.pallas_call(
+        functools.partial(spectra_kernel, seqs, share),
+        out_shape=jax.ShapeDtypeStruct(spread.shape, jnp.float32),
+        in_specs=[pl.BlockSpec(memory_space=pltpu.VMEM)] * 5,
+        out_specs=pl.BlockSpec(memory_space=pltpu.VMEM),
+        compiler_params=pltpu.CompilerParams(vmem_limit_bytes=48 * 2**20),
+        name="spectra",
+    )(spread, cos_turn, sin_turn, stack_table(forward_second), stack_table(inverse_second))
+    turned = turned.reshape(2 * outer, columns * LANES)
     rows = jnp.dot(inverse_first, turned, precision=lax.Precision.HIGH)
     return rows.reshape(outer, columns, LANES)
 

time: 74.7 us -> 70.2 us (0.940)
  Pallas kernels: 50.7 us -> 55.3 us
  matrix products: 10.2 us -> 6.3 us
  other arithmetic: 3.11 us -> 0.49 us
  local copies, waits for them, and re-layouts: 8.94 us -> 6.75 us
    pallas_call x0 -> x1, Pallas kernels: none -> 4.55 us  [convolve_all(): pl.pallas_call(functools.partial(spectra_kernel, seqs, share), out_shape=...]
    dot_general x2 -> x0, matrix products: 3.93 us -> none  [the longest x1 2.68 us: convolve_all(): part = jnp.dot(both, inverse_second, precision=lax.Precision.HIGH)]
    unnamed x30 -> x26, local copies, waits for them, and re-layouts: 4.45 us -> 2.3 us
    sub x2 -> x0, other arithmetic: 2.04 us -> none  [the longest x1 1.71 us: convolve_all(): mixed_real = value_real * kernel_real - value_imag * kernel_imag]
where the time goes in v3:
time: 70.2 us; the launch traced here: 69.9 us
  Pallas kernels  55.3 us (79%)
  local copies, waits for them, and re-layouts  6.75 us (10%)
  matrix products  6.3 us (9%)
  between operations  1.06 us (2%)
    pallas_call x2, Pallas kernels, exchange(): pl.pallas_call(functools.partial(exchange_kernel, count, seqs), out_shape...  36.4 us
    pallas_call x1, Pallas kernels, reduce_and_join(): pl.pallas_call(functools.partial(reduce_kernel, count), out_shape=(jax.Sh...  14.3 us
    pallas_call x1, Pallas kernels, convolve_all(): pl.pallas_call(functools.partial(spectra_kernel, seqs, share), out_shape=...  4.55 us
    dot_general x7, matrix products, contract(): lax.dot_general(left, right, (((left_dim,), (right_dim,)), ((), ())), pre...  3.48 us
    unnamed x26, local copies, waits for them, and re-layouts  2.3 us
    dot_general x1, matrix products, convolve_all(): rows = jnp.dot(inverse_first, turned, precision=lax.Precision.HIGH)  1.63 us

profile of v3, /device:TPU:0, one launch (start us, length us, event | category | flops | bytes accessed | tf_op | source)
XLA Modules:
  0.0 69.9 jit_solution(9056201101344555513)
XLA Ops:
  0.7 1.0 %dynamic-slice_bitcast_fusion = bf16[256,256]{0,1:T(8,128)(2,1)S(1)} fusion(bf16[512,256]{1,0:T(8,128)(2,1)} %param.21, s32[]{:T(128)S(6)} %select_n.3), kind=kLoop, calls=%fused_computation.39 | loop fusion | bytes 262148 | tf_op jit(solution)/shard_map/transpose | solution.py:317
  1.8 1.2 %convolution_convert_fusion = bf16[256,512]{1,0:T(8,128)(2,1)S(1)} fusion(bf16[256,256]{1,0:T(8,128)(2,1)} %param.18, bf16[1,512,256]{2,1,0:T(8,128)(2,1)S(1)} %copy-done), kind=kOutput, calls=%fused_computation.7 | convolution fusion | flops 67239936 | bytes 655360 | tf_op jit(solution)/shard_map/dot_general | solution.py:54
  3.0 0.2 reshape.88
  3.2 0.3 fusion.24
  3.5 0.3 multiply_convert_fusion.2
  3.7 0.2 reshape.89
  4.0 17.5 %exchange.2 = bf16[16,160,128]{2,1,0:T(8,128)(2,1)S(1)} custom-call(bf16[16,160,128]{2,1,0:T(8,128)(2,1)S(1)} %pad_maximum_fusion.sent), custom_call_target="tpu_custom_call" | custom-call | tf_op jit(solution)/shard_map/exchange/pallas_call | solution.py:109
  21.8 0.5 copy-done.11
  22.3 0.5 fusion.10
  22.7 0.2 copy-done.10
  23.0 0.5 fusion.3
  23.5 0.5 copy.34
  24.0 0.5 copy-done.1
  24.5 0.1 copy-done.2
  24.6 4.5 %spectra.1 = f32[64,80,128]{2,1,0:T(8,128)S(1)} custom-call(f32[64,80,128]{2,1,0:T(8,128)S(1)} %bitcast.90, f32[32,1,128]{2,1,0:T(1,128)S(1)} %copy-done.4, f32[32,1,128]{2,1,0:T(1,128)S(1)} %copy-done.3, bf16[768,256]{1,0:T(8,128)(2,1)S(1)} %copy-done.2, bf16[768,256]{1,0:T(8,128)(2,1)S(1)} %copy-done.1), custom_call_target="tpu_custom_call" | custom-call | tf_op jit(solution)/shard_map/spectra/pallas_call | solution.py:290
  29.2 1.6 %fusion.4 = f32[4,8,80,128]{3,1,2,0:T(8,128)S(1)} fusion(f32[32,64]{1,0:T(8,128)S(1)} %copy-done.9, f32[8,8,80,128]{3,2,1,0:T(8,128)S(1)} %bitcast.89), kind=kOutput, calls=%fused_computation.5 | convolution fusion | flops 125829120 | bytes 3940352 | tf_op jit(solution)/shard_map/dot_general | solution.py:299
  30.8 0.2 copy.36
  31.1 0.1 slice.38
  31.2 0.4 copy.27
  31.8 18.9 %exchange.3 = bf16[16,160,128]{2,1,0:T(8,128)(2,1)S(1)} custom-call(bf16[16,160,128]{2,1,0:T(8,128)(2,1)S(1)} %pad_maximum_fusion.2.sent), custom_call_target="tpu_custom_call" | custom-call | tf_op jit(solution)/shard_map/exchange/pallas_call | solution.py:109
  50.9 0.2 multiply_convert_fusion
  51.1 0.2 convolution_bitcast_fusion
  51.3 0.2 reshape.103
  51.5 0.3 fusion.22
  51.8 0.2 copy-done.6
  52.0 0.3 fusion.27
  52.2 1.0 %fusion.8 = bf16[1,512,256]{2,1,0:T(8,128)(2,1)} fusion(f32[512,256]{1,0:T(8,128)S(1)} %fusion.27, bf16[256,512]{1,0:T(8,128)(2,1)S(1)} %get-tuple-element.10, bf16[256,256]{1,0:T(8,128)(2,1)S(1)} %copy-done.7), kind=kOutput, calls=%fused_computation.9 | convolution fusion | flops 67371008 | bytes 1179648 | tf_op jit(solution)/shard_map/dot_general | solution.py:54
  53.2 0.3 fusion.20
  53.6 0.1 reshape.105.proj
  53.8 14.3 %reduce_and_join.1 = (f32[2,96,128]{2,1,0:T(8,128)S(1)}, bf16[2,512,128]{2,1,0:T(8,128)(2,1)S(1)}) custom-call(bf16[2,8,96,128]{3,2,1,0:T(8,128)(2,1)S(1)} %reshape.105.proj, bf16[512,128]{1,0:T(8,128)(2,1)S(1)} %bitcast.91), custom_call_target="tpu_custom_call" | custom-call | tf_op jit(solution)/shard_map/reduce_and_join/pallas_call | solution.py:203
  68.1 0.6 copy.30
  68.9 1.0 %copy.31 = f32[2,256,256]{2,1,0:T(8,128)} copy(f32[2,256,256]{1,2,0:T(8,128)S(1)} %bitcast.100) | data formatting | bytes 1048576 | tf_op jit(solution)/shard_map/convert_element_type | solution.py:377
  (37 shorter events, 1.0 us)
Async XLA Ops:
  0.6 1.2 %copy-start = (bf16[1,512,256]{2,1,0:T(8,128)(2,1)S(1)}, bf16[1,512,256]{2,1,0:T(8,128)(2,1)}, u32[]{:S(2)}) copy-start(bf16[1,512,256]{2,1,0:T(8,128)(2,1)} %param.17) | copy-start | bytes 786436
  0.6 2.5 %copy-start.7 = (bf16[256,256]{1,0:T(8,128)(2,1)S(1)}, bf16[256,256]{1,0:T(8,128)(2,1)}, u32[]{:S(2)}) copy-start(bf16[256,256]{1,0:T(8,128)(2,1)} %param.19) | copy-start | bytes 393220
  1.6 1.8 %copy-start.5 = (bf16[1,512,256]{2,1,0:T(8,128)(2,1)S(1)}, bf16[1,512,256]{2,1,0:T(8,128)(2,1)}, u32[]{:S(2)}) copy-start(bf16[1,512,256]{2,1,0:T(8,128)(2,1)} %param.22) | copy-start | bytes 786436
  1.6 1.8 %copy-start.8 = (bf16[256,256]{1,0:T(8,128)(2,1)S(1)}, bf16[256,256]{1,0:T(8,128)(2,1)}, u32[]{:S(2)}) copy-start(bf16[256,256]{1,0:T(8,128)(2,1)} %param.20) | copy-start | bytes 393220
  21.5 0.7 %copy-start.11 = (bf16[64,32]{1,0:T(8,128)(2,1)S(1)}, bf16[64,32]{1,0:T(8,128)(2,1)}, u32[]{:S(2)}) copy-start(bf16[64,32]{1,0:T(8,128)(2,1)} %constant.45) | copy-start | bytes 12292
  22.3 0.7 %copy-start.10 = (bf16[64,32]{1,0:T(8,128)(2,1)S(1)}, bf16[64,32]{1,0:T(8,128)(2,1)}, u32[]{:S(2)}) copy-start(bf16[64,32]{1,0:T(8,128)(2,1)} %constant.46) | copy-start | bytes 12292
  23.5 1.0 %copy-start.1 = (bf16[768,256]{1,0:T(8,128)(2,1)S(1)}, bf16[768,256]{1,0:T(8,128)(2,1)}, u32[]{:S(2)}) copy-start(bf16[768,256]{1,0:T(8,128)(2,1)} %constant.44.inverse) | copy-start | bytes 1179652
  23.5 1.1 %copy-start.2 = (bf16[768,256]{1,0:T(8,128)(2,1)S(1)}, bf16[768,256]{1,0:T(8,128)(2,1)}, u32[]{:S(2)}) copy-start(bf16[768,256]{1,0:T(8,128)(2,1)} %constant.43.forward) | copy-start | bytes 1179652
  23.5 1.1 %copy-start.3 = (f32[32,1,128]{2,1,0:T(1,128)S(1)}, f32[32,1,128]{2,1,0:T(1,128)}, u32[]{:S(2)}) copy-start(f32[32,1,128]{2,1,0:T(1,128)} %constant.38.clone.sin_ref) | copy-start | bytes 49156
  23.5 1.1 %copy-start.4 = (f32[32,1,128]{2,1,0:T(1,128)S(1)}, f32[32,1,128]{2,1,0:T(1,128)}, u32[]{:S(2)}) copy-start(f32[32,1,128]{2,1,0:T(1,128)} %constant.37.clone.cos_ref) | copy-start | bytes 49156
  24.6 4.6 %copy-start.9 = (f32[32,64]{1,0:T(8,128)S(1)}, f32[32,64]{1,0:T(8,128)}, u32[]{:S(2)}) copy-start(f32[32,64]{1,0:T(8,128)} %constant.39.clone) | copy-start | bytes 24580
  51.1 0.9 %copy-start.6 = (bf16[256,256]{1,0:T(8,128)(2,1)S(1)}, bf16[256,256]{1,0:T(8,128)(2,1)}, u32[]{:S(2)}) copy-start(bf16[256,256]{1,0:T(8,128)(2,1)} %param.18) | copy-start | bytes 393220

commit v4 on v3

--- a/solution.py
+++ b/solution.py
@@ -87,15 +87,16 @@
             device_id_type=pl.DeviceIdType.MESH,
         )
 
-    def launch(step, carry):
-        remote(step).start()
+    def launch(turn, carry):
+        away = lax.div(turn + 1, 2) * (1 - 2 * lax.rem(turn, 2))
+        remote(peers // 2 + away).start()
         return carry
 
     def finish(step, carry):
         remote(step).wait()
         return carry
 
-    lax.fori_loop(1, peers, launch, 0)
+    lax.fori_loop(0, peers - 1, launch, 0)
     own.wait()
     lax.fori_loop(1, peers, finish, 0)
 

time: 70.2 us -> 69.3 us (0.987)
  Pallas kernels: 55.3 us -> 54.3 us
    pallas_call x1, Pallas kernels: 14.3 us -> 11.5 us  [reduce_and_join(): pl.pallas_call(functools.partial(reduce_kernel, count), out_shape=(jax.Sh...]
    pallas_call x2, Pallas kernels: 36.4 us -> 38.3 us  [exchange(): pl.pallas_call(functools.partial(exchange_kernel, count, seqs), out_shape...]
where the time goes in v4:
time: 69.3 us; the launch traced here: 68.9 us
  Pallas kernels  54.3 us (78%)
  local copies, waits for them, and re-layouts  6.75 us (10%)
  matrix products  6.29 us (9%)
  between operations  1.06 us (2%)
    pallas_call x2, Pallas kernels, exchange(): pl.pallas_call(functools.partial(exchange_kernel, count, seqs), out_shape...  38.3 us
    pallas_call x1, Pallas kernels, reduce_and_join(): pl.pallas_call(functools.partial(reduce_kernel, count), out_shape=(jax.Sh...  11.5 us
    pallas_call x1, Pallas kernels, convolve_all(): pl.pallas_call(functools.partial(spectra_kernel, seqs, share), out_shape=...  4.55 us
    dot_general x7, matrix products, contract(): lax.dot_general(left, right, (((left_dim,), (right_dim,)), ((), ())), pre...  3.48 us
    unnamed x26, local copies, waits for them, and re-layouts  2.3 us
    dot_general x1, matrix products, convolve_all(): rows = jnp.dot(inverse_first, turned, precision=lax.Precision.HIGH)  1.63 us

profile of v4, /device:TPU:0, one launch (start us, length us, event | category | flops | bytes accessed | tf_op | source)
XLA Modules:
  0.0 68.9 jit_solution(9205228212607018664)
XLA Ops:
  0.7 1.0 %dynamic-slice_bitcast_fusion = bf16[256,256]{0,1:T(8,128)(2,1)S(1)} fusion(bf16[512,256]{1,0:T(8,128)(2,1)} %param.21, s32[]{:T(128)S(6)} %select_n.3), kind=kLoop, calls=%fused_computation.39 | loop fusion | bytes 262148 | tf_op jit(solution)/shard_map/transpose | solution.py:318
  1.8 1.2 %convolution_convert_fusion = bf16[256,512]{1,0:T(8,128)(2,1)S(1)} fusion(bf16[256,256]{1,0:T(8,128)(2,1)} %param.18, bf16[1,512,256]{2,1,0:T(8,128)(2,1)S(1)} %copy-done), kind=kOutput, calls=%fused_computation.7 | convolution fusion | flops 67239936 | bytes 655360 | tf_op jit(solution)/shard_map/dot_general | solution.py:54
  3.0 0.2 reshape.88
  3.2 0.3 fusion.24
  3.5 0.3 multiply_convert_fusion.2
  3.7 0.2 reshape.89
  4.0 20.2 %exchange.2 = bf16[16,160,128]{2,1,0:T(8,128)(2,1)S(1)} custom-call(bf16[16,160,128]{2,1,0:T(8,128)(2,1)S(1)} %pad_maximum_fusion.sent), custom_call_target="tpu_custom_call" | custom-call | tf_op jit(solution)/shard_map/exchange/pallas_call | solution.py:110
  24.4 0.5 copy-done.11
  24.9 0.5 fusion.10
  25.4 0.2 copy-done.10
  25.6 0.5 fusion.3
  26.2 0.5 copy.34
  26.7 0.5 copy-done.1
  27.1 0.1 copy-done.2
  27.3 4.5 %spectra.1 = f32[64,80,128]{2,1,0:T(8,128)S(1)} custom-call(f32[64,80,128]{2,1,0:T(8,128)S(1)} %bitcast.90, f32[32,1,128]{2,1,0:T(1,128)S(1)} %copy-done.4, f32[32,1,128]{2,1,0:T(1,128)S(1)} %copy-done.3, bf16[768,256]{1,0:T(8,128)(2,1)S(1)} %copy-done.2, bf16[768,256]{1,0:T(8,128)(2,1)S(1)} %copy-done.1), custom_call_target="tpu_custom_call" | custom-call | tf_op jit(solution)/shard_map/spectra/pallas_call | solution.py:291
  31.8 1.6 %fusion.4 = f32[4,8,80,128]{3,1,2,0:T(8,128)S(1)} fusion(f32[32,64]{1,0:T(8,128)S(1)} %copy-done.9, f32[8,8,80,128]{3,2,1,0:T(8,128)S(1)} %bitcast.89), kind=kOutput, calls=%fused_computation.5 | convolution fusion | flops 125829120 | bytes 3940352 | tf_op jit(solution)/shard_map/dot_general | solution.py:300
  33.5 0.2 copy.36
  33.7 0.1 slice.38
  33.9 0.4 copy.27
  34.5 18.1 %exchange.3 = bf16[16,160,128]{2,1,0:T(8,128)(2,1)S(1)} custom-call(bf16[16,160,128]{2,1,0:T(8,128)(2,1)S(1)} %pad_maximum_fusion.2.sent), custom_call_target="tpu_custom_call" | custom-call | tf_op jit(solution)/shard_map/exchange/pallas_call | solution.py:110
  52.8 0.2 multiply_convert_fusion
  53.0 0.2 convolution_bitcast_fusion
  53.2 0.2 reshape.103
  53.4 0.3 fusion.22
  53.7 0.2 copy-done.6
  53.9 0.3 fusion.27
  54.2 1.0 %fusion.8 = bf16[1,512,256]{2,1,0:T(8,128)(2,1)} fusion(f32[512,256]{1,0:T(8,128)S(1)} %fusion.27, bf16[256,512]{1,0:T(8,128)(2,1)S(1)} %get-tuple-element.10, bf16[256,256]{1,0:T(8,128)(2,1)S(1)} %copy-done.7), kind=kOutput, calls=%fused_computation.9 | convolution fusion | flops 67371008 | bytes 1179648 | tf_op jit(solution)/shard_map/dot_general | solution.py:54
  55.1 0.3 fusion.20
  55.5 0.1 reshape.105.proj
  55.7 11.5 %reduce_and_join.1 = (f32[2,96,128]{2,1,0:T(8,128)S(1)}, bf16[2,512,128]{2,1,0:T(8,128)(2,1)S(1)}) custom-call(bf16[2,8,96,128]{3,2,1,0:T(8,128)(2,1)S(1)} %reshape.105.proj, bf16[512,128]{1,0:T(8,128)(2,1)S(1)} %bitcast.91), custom_call_target="tpu_custom_call" | custom-call | tf_op jit(solution)/shard_map/reduce_and_join/pallas_call | solution.py:204
  67.2 0.6 copy.30
  67.9 1.0 %copy.31 = f32[2,256,256]{2,1,0:T(8,128)} copy(f32[2,256,256]{1,2,0:T(8,128)S(1)} %bitcast.100) | data formatting | bytes 1048576 | tf_op jit(solution)/shard_map/convert_element_type | solution.py:378
  (37 shorter events, 1.0 us)
Async XLA Ops:
  0.6 1.2 %copy-start = (bf16[1,512,256]{2,1,0:T(8,128)(2,1)S(1)}, bf16[1,512,256]{2,1,0:T(8,128)(2,1)}, u32[]{:S(2)}) copy-start(bf16[1,512,256]{2,1,0:T(8,128)(2,1)} %param.17) | copy-start | bytes 786436
  0.6 2.5 %copy-start.7 = (bf16[256,256]{1,0:T(8,128)(2,1)S(1)}, bf16[256,256]{1,0:T(8,128)(2,1)}, u32[]{:S(2)}) copy-start(bf16[256,256]{1,0:T(8,128)(2,1)} %param.19) | copy-start | bytes 393220
  1.6 1.8 %copy-start.5 = (bf16[1,512,256]{2,1,0:T(8,128)(2,1)S(1)}, bf16[1,512,256]{2,1,0:T(8,128)(2,1)}, u32[]{:S(2)}) copy-start(bf16[1,512,256]{2,1,0:T(8,128)(2,1)} %param.22) | copy-start | bytes 786436
  1.6 1.8 %copy-start.8 = (bf16[256,256]{1,0:T(8,128)(2,1)S(1)}, bf16[256,256]{1,0:T(8,128)(2,1)}, u32[]{:S(2)}) copy-start(bf16[256,256]{1,0:T(8,128)(2,1)} %param.20) | copy-start | bytes 393220
  24.2 0.7 %copy-start.11 = (bf16[64,32]{1,0:T(8,128)(2,1)S(1)}, bf16[64,32]{1,0:T(8,128)(2,1)}, u32[]{:S(2)}) copy-start(bf16[64,32]{1,0:T(8,128)(2,1)} %constant.45) | copy-start | bytes 12292
  24.9 0.7 %copy-start.10 = (bf16[64,32]{1,0:T(8,128)(2,1)S(1)}, bf16[64,32]{1,0:T(8,128)(2,1)}, u32[]{:S(2)}) copy-start(bf16[64,32]{1,0:T(8,128)(2,1)} %constant.46) | copy-start | bytes 12292
  26.1 1.0 %copy-start.1 = (bf16[768,256]{1,0:T(8,128)(2,1)S(1)}, bf16[768,256]{1,0:T(8,128)(2,1)}, u32[]{:S(2)}) copy-start(bf16[768,256]{1,0:T(8,128)(2,1)} %constant.44.inverse) | copy-start | bytes 1179652
  26.2 1.1 %copy-start.2 = (bf16[768,256]{1,0:T(8,128)(2,1)S(1)}, bf16[768,256]{1,0:T(8,128)(2,1)}, u32[]{:S(2)}) copy-start(bf16[768,256]{1,0:T(8,128)(2,1)} %constant.43.forward) | copy-start | bytes 1179652
  26.2 1.1 %copy-start.3 = (f32[32,1,128]{2,1,0:T(1,128)S(1)}, f32[32,1,128]{2,1,0:T(1,128)}, u32[]{:S(2)}) copy-start(f32[32,1,128]{2,1,0:T(1,128)} %constant.38.clone.sin_ref) | copy-start | bytes 49156
  26.2 1.1 %copy-start.4 = (f32[32,1,128]{2,1,0:T(1,128)S(1)}, f32[32,1,128]{2,1,0:T(1,128)}, u32[]{:S(2)}) copy-start(f32[32,1,128]{2,1,0:T(1,128)} %constant.37.clone.cos_ref) | copy-start | bytes 49156
  27.3 4.6 %copy-start.9 = (f32[32,64]{1,0:T(8,128)S(1)}, f32[32,64]{1,0:T(8,128)}, u32[]{:S(2)}) copy-start(f32[32,64]{1,0:T(8,128)} %constant.39.clone) | copy-start | bytes 24580
  53.0 0.9 %copy-start.6 = (bf16[256,256]{1,0:T(8,128)(2,1)S(1)}, bf16[256,256]{1,0:T(8,128)(2,1)}, u32[]{:S(2)}) copy-start(bf16[256,256]{1,0:T(8,128)(2,1)} %param.18) | copy-start | bytes 393220

commit v5 on v4

--- a/solution.py
+++ b/solution.py
@@ -160,7 +160,27 @@
         )
         return carry
 
-    def launch(step, carry):
+    def outwards(turn):
+        return count // 2 + lax.div(turn + 1, 2) * (1 - 2 * lax.rem(turn, 2))
+
+    def half(step):
+        peer = lax.rem(place + step, count)
+        return send(proj.at[1 - core, peer], other.at[peer], step)
+
+    def offer(turn, carry):
+        half(outwards(turn)).start()
+        return carry
+
+    def join(step):
+        half(step).wait()
+        peer = lax.rem(place + step, count)
+        stage[peer] = (
+            proj[core, peer].astype(jnp.float32) + other[peer].astype(jnp.float32)
+        ).astype(jnp.bfloat16)
+
+    def launch(turn, carry):
+        step = outwards(turn)
+        join(step)
         across(step).start()
         return carry
 
@@ -176,20 +196,16 @@
     )
     lax.fori_loop(1, count, greet, 0)
     pl.semaphore_wait(barrier, count)
-    halves = send(proj.at[1 - core], other, 0)
-    halves.start()
-    taps = send(terms, all_terms.at[core], 1)
+    lax.fori_loop(0, count, offer, 0)
+    taps = send(terms, all_terms.at[core], count)
     taps.start()
     all_terms[core] = terms[...]
-    halves.wait()
-    stage[...] = (proj[core].astype(jnp.float32) + other[...].astype(jnp.float32)).astype(
-        jnp.bfloat16
-    )
-    lax.fori_loop(1, count, launch, 0)
+    lax.fori_loop(0, count - 1, launch, 0)
+    join(0)
     taps.wait()
     lax.fori_loop(1, count, finish, 0)
     sums[core] = lax.fori_loop(1, count, add, stage[place].astype(jnp.float32))
-    total = send(sums.at[core], sums.at[core], 2)
+    total = send(sums.at[core], sums.at[core], count + 1)
     total.start()
     total.wait()
 
@@ -213,8 +229,8 @@
             pltpu.VMEM(part, jnp.bfloat16),
             pltpu.VMEM(part, jnp.bfloat16),
             pltpu.VMEM(part, jnp.bfloat16),
-            pltpu.SemaphoreType.DMA((3,)),
-            pltpu.SemaphoreType.DMA((3,)),
+            pltpu.SemaphoreType.DMA((count + 2,)),
+            pltpu.SemaphoreType.DMA((count + 2,)),
             pltpu.SemaphoreType.DMA((count,)),
             pltpu.SemaphoreType.DMA((count,)),
         ],

time: 69.3 us -> 70.8 us (1.022)
  Pallas kernels: 54.3 us -> 55.8 us
    pallas_call x1, Pallas kernels: 11.5 us -> 13 us  [reduce_and_join(): pl.pallas_call(functools.partial(reduce_kernel, count), out_shape=(jax.Sh...]
where the time goes in v5:
time: 70.8 us; the launch traced here: 70.4 us
  Pallas kernels  55.8 us (79%)
  local copies, waits for them, and re-layouts  6.75 us (10%)
  matrix products  6.29 us (9%)
  between operations  1.06 us (1%)
    pallas_call x2, Pallas kernels, exchange(): pl.pallas_call(functools.partial(exchange_kernel, count, seqs), out_shape...  38.3 us
    pallas_call x1, Pallas kernels, reduce_and_join(): pl.pallas_call(functools.partial(reduce_kernel, count), out_shape=(jax.Sh...  13 us
    pallas_call x1, Pallas kernels, convolve_all(): pl.pallas_call(functools.partial(spectra_kernel, seqs, share), out_shape=...  4.55 us
    dot_general x7, matrix products, contract(): lax.dot_general(left, right, (((left_dim,), (right_dim,)), ((), ())), pre...  3.48 us
    unnamed x26, local copies, waits for them, and re-layouts  2.3 us
    dot_general x1, matrix products, convolve_all(): rows = jnp.dot(inverse_first, turned, precision=lax.Precision.HIGH)  1.63 us

profile of v5, /device:TPU:0, one launch (start us, length us, event | category | flops | bytes accessed | tf_op | source)
XLA Modules:
  0.0 70.4 jit_solution(8460374118522933120)
XLA Ops:
  0.7 1.0 %dynamic-slice_bitcast_fusion = bf16[256,256]{0,1:T(8,128)(2,1)S(1)} fusion(bf16[512,256]{1,0:T(8,128)(2,1)} %param.21, s32[]{:T(128)S(6)} %select_n.3), kind=kLoop, calls=%fused_computation.39 | loop fusion | bytes 262148 | tf_op jit(solution)/shard_map/transpose | solution.py:334
  1.8 1.2 %convolution_convert_fusion = bf16[256,512]{1,0:T(8,128)(2,1)S(1)} fusion(bf16[256,256]{1,0:T(8,128)(2,1)} %param.18, bf16[1,512,256]{2,1,0:T(8,128)(2,1)S(1)} %copy-done), kind=kOutput, calls=%fused_computation.7 | convolution fusion | flops 67239936 | bytes 655360 | tf_op jit(solution)/shard_map/dot_general | solution.py:54
  3.0 0.2 reshape.88
  3.2 0.3 fusion.24
  3.5 0.3 multiply_convert_fusion.2
  3.7 0.2 reshape.89
  4.0 20.2 %exchange.2 = bf16[16,160,128]{2,1,0:T(8,128)(2,1)S(1)} custom-call(bf16[16,160,128]{2,1,0:T(8,128)(2,1)S(1)} %pad_maximum_fusion.sent), custom_call_target="tpu_custom_call" | custom-call | tf_op jit(solution)/shard_map/exchange/pallas_call | solution.py:110
  24.4 0.5 copy-done.11
  24.9 0.5 fusion.10
  25.4 0.2 copy-done.10
  25.6 0.5 fusion.3
  26.2 0.5 copy.34
  26.7 0.5 copy-done.1
  27.1 0.1 copy-done.2
  27.3 4.5 %spectra.1 = f32[64,80,128]{2,1,0:T(8,128)S(1)} custom-call(f32[64,80,128]{2,1,0:T(8,128)S(1)} %bitcast.90, f32[32,1,128]{2,1,0:T(1,128)S(1)} %copy-done.4, f32[32,1,128]{2,1,0:T(1,128)S(1)} %copy-done.3, bf16[768,256]{1,0:T(8,128)(2,1)S(1)} %copy-done.2, bf16[768,256]{1,0:T(8,128)(2,1)S(1)} %copy-done.1), custom_call_target="tpu_custom_call" | custom-call | tf_op jit(solution)/shard_map/spectra/pallas_call | solution.py:307
  31.8 1.6 %fusion.4 = f32[4,8,80,128]{3,1,2,0:T(8,128)S(1)} fusion(f32[32,64]{1,0:T(8,128)S(1)} %copy-done.9, f32[8,8,80,128]{3,2,1,0:T(8,128)S(1)} %bitcast.89), kind=kOutput, calls=%fused_computation.5 | convolution fusion | flops 125829120 | bytes 3940352 | tf_op jit(solution)/shard_map/dot_general | solution.py:316
  33.5 0.2 copy.36
  33.7 0.1 slice.38
  33.9 0.4 copy.27
  34.5 18.1 %exchange.3 = bf16[16,160,128]{2,1,0:T(8,128)(2,1)S(1)} custom-call(bf16[16,160,128]{2,1,0:T(8,128)(2,1)S(1)} %pad_maximum_fusion.2.sent), custom_call_target="tpu_custom_call" | custom-call | tf_op jit(solution)/shard_map/exchange/pallas_call | solution.py:110
  52.8 0.2 multiply_convert_fusion
  53.0 0.2 convolution_bitcast_fusion
  53.2 0.2 reshape.103
  53.4 0.3 fusion.22
  53.7 0.2 copy-done.6
  53.9 0.3 fusion.27
  54.2 1.0 %fusion.8 = bf16[1,512,256]{2,1,0:T(8,128)(2,1)} fusion(f32[512,256]{1,0:T(8,128)S(1)} %fusion.27, bf16[256,512]{1,0:T(8,128)(2,1)S(1)} %get-tuple-element.10, bf16[256,256]{1,0:T(8,128)(2,1)S(1)} %copy-done.7), kind=kOutput, calls=%fused_computation.9 | convolution fusion | flops 67371008 | bytes 1179648 | tf_op jit(solution)/shard_map/dot_general | solution.py:54
  55.1 0.3 fusion.20
  55.5 0.1 reshape.105.proj
  55.7 13.0 %reduce_and_join.1 = (f32[2,96,128]{2,1,0:T(8,128)S(1)}, bf16[2,512,128]{2,1,0:T(8,128)(2,1)S(1)}) custom-call(bf16[2,8,96,128]{3,2,1,0:T(8,128)(2,1)S(1)} %reshape.105.proj, bf16[512,128]{1,0:T(8,128)(2,1)S(1)} %bitcast.91), custom_call_target="tpu_custom_call" | custom-call | tf_op jit(solution)/shard_map/reduce_and_join/pallas_call | solution.py:220
  68.7 0.6 copy.30
  69.4 1.0 %copy.31 = f32[2,256,256]{2,1,0:T(8,128)} copy(f32[2,256,256]{1,2,0:T(8,128)S(1)} %bitcast.100) | data formatting | bytes 1048576 | tf_op jit(solution)/shard_map/convert_element_type | solution.py:394
  (37 shorter events, 1.0 us)
Async XLA Ops:
  0.6 1.2 %copy-start = (bf16[1,512,256]{2,1,0:T(8,128)(2,1)S(1)}, bf16[1,512,256]{2,1,0:T(8,128)(2,1)}, u32[]{:S(2)}) copy-start(bf16[1,512,256]{2,1,0:T(8,128)(2,1)} %param.17) | copy-start | bytes 786436
  0.6 2.5 %copy-start.7 = (bf16[256,256]{1,0:T(8,128)(2,1)S(1)}, bf16[256,256]{1,0:T(8,128)(2,1)}, u32[]{:S(2)}) copy-start(bf16[256,256]{1,0:T(8,128)(2,1)} %param.19) | copy-start | bytes 393220
  1.6 1.8 %copy-start.5 = (bf16[1,512,256]{2,1,0:T(8,128)(2,1)S(1)}, bf16[1,512,256]{2,1,0:T(8,128)(2,1)}, u32[]{:S(2)}) copy-start(bf16[1,512,256]{2,1,0:T(8,128)(2,1)} %param.22) | copy-start | bytes 786436
  1.6 1.8 %copy-start.8 = (bf16[256,256]{1,0:T(8,128)(2,1)S(1)}, bf16[256,256]{1,0:T(8,128)(2,1)}, u32[]{:S(2)}) copy-start(bf16[256,256]{1,0:T(8,128)(2,1)} %param.20) | copy-start | bytes 393220
  24.2 0.7 %copy-start.11 = (bf16[64,32]{1,0:T(8,128)(2,1)S(1)}, bf16[64,32]{1,0:T(8,128)(2,1)}, u32[]{:S(2)}) copy-start(bf16[64,32]{1,0:T(8,128)(2,1)} %constant.45) | copy-start | bytes 12292
  24.9 0.7 %copy-start.10 = (bf16[64,32]{1,0:T(8,128)(2,1)S(1)}, bf16[64,32]{1,0:T(8,128)(2,1)}, u32[]{:S(2)}) copy-start(bf16[64,32]{1,0:T(8,128)(2,1)} %constant.46) | copy-start | bytes 12292
  26.1 1.0 %copy-start.1 = (bf16[768,256]{1,0:T(8,128)(2,1)S(1)}, bf16[768,256]{1,0:T(8,128)(2,1)}, u32[]{:S(2)}) copy-start(bf16[768,256]{1,0:T(8,128)(2,1)} %constant.44.inverse) | copy-start | bytes 1179652
  26.2 1.1 %copy-start.2 = (bf16[768,256]{1,0:T(8,128)(2,1)S(1)}, bf16[768,256]{1,0:T(8,128)(2,1)}, u32[]{:S(2)}) copy-start(bf16[768,256]{1,0:T(8,128)(2,1)} %constant.43.forward) | copy-start | bytes 1179652
  26.2 1.1 %copy-start.3 = (f32[32,1,128]{2,1,0:T(1,128)S(1)}, f32[32,1,128]{2,1,0:T(1,128)}, u32[]{:S(2)}) copy-start(f32[32,1,128]{2,1,0:T(1,128)} %constant.38.clone.sin_ref) | copy-start | bytes 49156
  26.2 1.1 %copy-start.4 = (f32[32,1,128]{2,1,0:T(1,128)S(1)}, f32[32,1,128]{2,1,0:T(1,128)}, u32[]{:S(2)}) copy-start(f32[32,1,128]{2,1,0:T(1,128)} %constant.37.clone.cos_ref) | copy-start | bytes 49156
  27.3 4.6 %copy-start.9 = (f32[32,64]{1,0:T(8,128)S(1)}, f32[32,64]{1,0:T(8,128)}, u32[]{:S(2)}) copy-start(f32[32,64]{1,0:T(8,128)} %constant.39.clone) | copy-start | bytes 24580
  53.0 0.9 %copy-start.6 = (bf16[256,256]{1,0:T(8,128)(2,1)S(1)}, bf16[256,256]{1,0:T(8,128)(2,1)}, u32[]{:S(2)}) copy-start(bf16[256,256]{1,0:T(8,128)(2,1)} %param.18) | copy-start | bytes 393220

commit v6 on v4

--- a/solution.py
+++ b/solution.py
@@ -271,8 +271,8 @@
             jnp.concatenate(mixed_imags + back_imags + [corr_imag], axis=1),
             inverse,
         )
-        turned[upper] = real * cos_turn - imag * sin_turn
-        turned[lower] = imag * cos_turn + real * sin_turn
+        turned[upper] = (real * cos_turn - imag * sin_turn).astype(jnp.bfloat16)
+        turned[lower] = (imag * cos_turn + real * sin_turn).astype(jnp.bfloat16)
         return carry
 
     lax.fori_loop(0, outer // chunk, step, 0)
@@ -290,14 +290,15 @@
     spread = spread.reshape(2 * outer, columns, LANES)
     turned = pl.pallas_call(
         functools.partial(spectra_kernel, seqs, share),
-        out_shape=jax.ShapeDtypeStruct(spread.shape, jnp.float32),
+        out_shape=jax.ShapeDtypeStruct(spread.shape, jnp.bfloat16),
         in_specs=[pl.BlockSpec(memory_space=pltpu.VMEM)] * 5,
         out_specs=pl.BlockSpec(memory_space=pltpu.VMEM),
         compiler_params=pltpu.CompilerParams(vmem_limit_bytes=48 * 2**20),
         name="spectra",
     )(spread, cos_turn, sin_turn, stack_table(forward_second), stack_table(inverse_second))
     turned = turned.reshape(2 * outer, columns * LANES)
-    rows = jnp.dot(inverse_first, turned, precision=lax.Precision.HIGH)
+    high, low = split_table(inverse_first)
+    rows = dot(jnp.concatenate([high, low], axis=1), jnp.concatenate([turned, turned], axis=0))
     return rows.reshape(outer, columns, LANES)
 
 

time: 69.3 us -> 68.7 us (level)
  matrix products: 6.29 us -> 5.38 us
    dot_general x1 -> x0, matrix products: 1.63 us -> none  [convolve_all(): rows = jnp.dot(inverse_first, turned, precision=lax.Precision.HIGH)]
    dot_general x3 -> x5, matrix products: 1.19 us -> 1.9 us  [dot(): return jnp.dot(left, right, preferred_element_type=jnp.float32)]
    unnamed x26 -> x28, local copies, waits for them, and re-layouts: 2.3 us -> 2.64 us
where the time goes in v6:
time: 68.7 us; the launch traced here: 68.3 us
  Pallas kernels  54.3 us (79%)
  local copies, waits for them, and re-layouts  7.09 us (10%)
  matrix products  5.38 us (8%)
  between operations  1.07 us (2%)
    pallas_call x2, Pallas kernels, exchange(): pl.pallas_call(functools.partial(exchange_kernel, count, seqs), out_shape...  38.3 us
    pallas_call x1, Pallas kernels, reduce_and_join(): pl.pallas_call(functools.partial(reduce_kernel, count), out_shape=(jax.Sh...  11.5 us
    pallas_call x1, Pallas kernels, convolve_all(): pl.pallas_call(functools.partial(spectra_kernel, seqs, share), out_shape=...  4.55 us
    dot_general x7, matrix products, contract(): lax.dot_general(left, right, (((left_dim,), (right_dim,)), ((), ())), pre...  3.48 us
    unnamed x28, local copies, waits for them, and re-layouts  2.64 us
    dot_general x5, matrix products, dot(): return jnp.dot(left, right, preferred_element_type=jnp.float32)  1.9 us

profile of v6, /device:TPU:0, one launch (start us, length us, event | category | flops | bytes accessed | tf_op | source)
XLA Modules:
  0.0 68.3 jit_solution(9432405654286328537)
XLA Ops:
  0.7 1.0 %dynamic-slice_bitcast_fusion = bf16[256,256]{0,1:T(8,128)(2,1)S(1)} fusion(bf16[512,256]{1,0:T(8,128)(2,1)} %param.22, s32[]{:T(128)S(6)} %select_n.3), kind=kLoop, calls=%fused_computation.42 | loop fusion | bytes 262148 | tf_op jit(solution)/shard_map/transpose | solution.py:319
  1.8 1.2 %convolution_convert_fusion = bf16[256,512]{1,0:T(8,128)(2,1)S(1)} fusion(bf16[256,256]{1,0:T(8,128)(2,1)} %param.19, bf16[1,512,256]{2,1,0:T(8,128)(2,1)S(1)} %copy-done), kind=kOutput, calls=%fused_computation.8 | convolution fusion | flops 67239936 | bytes 655360 | tf_op jit(solution)/shard_map/dot_general | solution.py:54
  3.0 0.2 reshape.88
  3.2 0.3 fusion.24
  3.5 0.3 multiply_convert_fusion.2
  3.7 0.2 reshape.89
  4.0 20.2 %exchange.2 = bf16[16,160,128]{2,1,0:T(8,128)(2,1)S(1)} custom-call(bf16[16,160,128]{2,1,0:T(8,128)(2,1)S(1)} %pad_maximum_fusion.sent), custom_call_target="tpu_custom_call" | custom-call | tf_op jit(solution)/shard_map/exchange/pallas_call | solution.py:110
  24.4 0.5 copy-done.10
  24.9 0.5 fusion.10
  25.4 0.2 copy-done.9
  25.6 0.5 fusion
  26.2 0.5 copy.35
  26.7 0.5 copy-done.1
  27.3 4.6 %spectra.1 = bf16[64,80,128]{2,1,0:T(8,128)(2,1)S(1)} custom-call(f32[64,80,128]{2,1,0:T(8,128)S(1)} %bitcast.92, f32[32,1,128]{2,1,0:T(1,128)S(1)} %copy-done.4, f32[32,1,128]{2,1,0:T(1,128)S(1)} %copy-done.3, bf16[768,256]{1,0:T(8,128)(2,1)S(1)} %copy-done.2, bf16[768,256]{1,0:T(8,128)(2,1)S(1)} %copy-done.1), custom_call_target="tpu_custom_call" | custom-call | tf_op jit(solution)/shard_map/spectra/pallas_call | solution.py:291
  31.8 0.4 fusion.2
  32.2 0.3 copy-done.11
  32.5 0.4 fusion.1
  32.9 0.2 copy.37
  33.3 0.4 copy.28
  33.9 18.1 %exchange.3 = bf16[16,160,128]{2,1,0:T(8,128)(2,1)S(1)} custom-call(bf16[16,160,128]{2,1,0:T(8,128)(2,1)S(1)} %pad_maximum_fusion.2.sent), custom_call_target="tpu_custom_call" | custom-call | tf_op jit(solution)/shard_map/exchange/pallas_call | solution.py:110
  52.2 0.2 multiply_convert_fusion
  52.4 0.2 convolution_bitcast_fusion
  52.7 0.2 reshape.103
  52.8 0.3 fusion.22
  53.1 0.2 copy-done.6
  53.3 0.3 fusion.27
  53.6 1.0 %fusion.6 = bf16[1,512,256]{2,1,0:T(8,128)(2,1)} fusion(f32[512,256]{1,0:T(8,128)S(1)} %fusion.27, bf16[256,512]{1,0:T(8,128)(2,1)S(1)} %get-tuple-element.10, bf16[256,256]{1,0:T(8,128)(2,1)S(1)} %copy-done.7), kind=kOutput, calls=%fused_computation.10 | convolution fusion | flops 67371008 | bytes 1179648 | tf_op jit(solution)/shard_map/dot_general | solution.py:54
  54.6 0.3 fusion.20
  55.0 0.1 reshape.105.proj
  55.1 11.5 %reduce_and_join.1 = (f32[2,96,128]{2,1,0:T(8,128)S(1)}, bf16[2,512,128]{2,1,0:T(8,128)(2,1)S(1)}) custom-call(bf16[2,8,96,128]{3,2,1,0:T(8,128)(2,1)S(1)} %reshape.105.proj, bf16[512,128]{1,0:T(8,128)(2,1)S(1)} %bitcast.93), custom_call_target="tpu_custom_call" | custom-call | tf_op jit(solution)/shard_map/reduce_and_join/pallas_call | solution.py:204
  66.6 0.6 copy.31
  67.3 1.0 %copy.32 = f32[2,256,256]{2,1,0:T(8,128)} copy(f32[2,256,256]{1,2,0:T(8,128)S(1)} %bitcast.102) | data formatting | bytes 1048576 | tf_op jit(solution)/shard_map/convert_element_type | solution.py:379
  (40 shorter events, 1.3 us)
Async XLA Ops:
  0.6 1.2 %copy-start = (bf16[1,512,256]{2,1,0:T(8,128)(2,1)S(1)}, bf16[1,512,256]{2,1,0:T(8,128)(2,1)}, u32[]{:S(2)}) copy-start(bf16[1,512,256]{2,1,0:T(8,128)(2,1)} %param.18) | copy-start | bytes 786436
  0.6 2.5 %copy-start.7 = (bf16[256,256]{1,0:T(8,128)(2,1)S(1)}, bf16[256,256]{1,0:T(8,128)(2,1)}, u32[]{:S(2)}) copy-start(bf16[256,256]{1,0:T(8,128)(2,1)} %param.20) | copy-start | bytes 393220
  1.6 1.8 %copy-start.5 = (bf16[1,512,256]{2,1,0:T(8,128)(2,1)S(1)}, bf16[1,512,256]{2,1,0:T(8,128)(2,1)}, u32[]{:S(2)}) copy-start(bf16[1,512,256]{2,1,0:T(8,128)(2,1)} %param.23) | copy-start | bytes 786436
  1.6 1.8 %copy-start.8 = (bf16[256,256]{1,0:T(8,128)(2,1)S(1)}, bf16[256,256]{1,0:T(8,128)(2,1)}, u32[]{:S(2)}) copy-start(bf16[256,256]{1,0:T(8,128)(2,1)} %param.21) | copy-start | bytes 393220
  24.2 0.7 %copy-start.10 = (bf16[64,32]{1,0:T(8,128)(2,1)S(1)}, bf16[64,32]{1,0:T(8,128)(2,1)}, u32[]{:S(2)}) copy-start(bf16[64,32]{1,0:T(8,128)(2,1)} %constant.50) | copy-start | bytes 12292
  24.9 0.7 %copy-start.9 = (bf16[64,32]{1,0:T(8,128)(2,1)S(1)}, bf16[64,32]{1,0:T(8,128)(2,1)}, u32[]{:S(2)}) copy-start(bf16[64,32]{1,0:T(8,128)(2,1)} %constant.51) | copy-start | bytes 12292
  26.1 1.0 %copy-start.1 = (bf16[768,256]{1,0:T(8,128)(2,1)S(1)}, bf16[768,256]{1,0:T(8,128)(2,1)}, u32[]{:S(2)}) copy-start(bf16[768,256]{1,0:T(8,128)(2,1)} %constant.48.inverse) | copy-start | bytes 1179652
  26.2 1.1 %copy-start.2 = (bf16[768,256]{1,0:T(8,128)(2,1)S(1)}, bf16[768,256]{1,0:T(8,128)(2,1)}, u32[]{:S(2)}) copy-start(bf16[768,256]{1,0:T(8,128)(2,1)} %constant.47.forward) | copy-start | bytes 1179652
  26.2 1.1 %copy-start.3 = (f32[32,1,128]{2,1,0:T(1,128)S(1)}, f32[32,1,128]{2,1,0:T(1,128)}, u32[]{:S(2)}) copy-start(f32[32,1,128]{2,1,0:T(1,128)} %constant.40.clone.sin_ref) | copy-start | bytes 49156
  26.2 1.1 %copy-start.4 = (f32[32,1,128]{2,1,0:T(1,128)S(1)}, f32[32,1,128]{2,1,0:T(1,128)}, u32[]{:S(2)}) copy-start(f32[32,1,128]{2,1,0:T(1,128)} %constant.39.clone.cos_ref) | copy-start | bytes 49156
  27.3 4.6 %copy-start.12 = (bf16[32,64]{1,0:T(8,128)(2,1)S(1)}, bf16[32,64]{1,0:T(8,128)(2,1)}, u32[]{:S(2)}) copy-start(bf16[32,64]{1,0:T(8,128)(2,1)} %constant.49) | copy-start | bytes 12292
  31.8 0.7 %copy-start.11 = (bf16[32,64]{1,0:T(8,128)(2,1)S(1)}, bf16[32,64]{1,0:T(8,128)(2,1)}, u32[]{:S(2)}) copy-start(bf16[32,64]{1,0:T(8,128)(2,1)} %constant.52) | copy-start | bytes 12292
  52.4 0.9 %copy-start.6 = (bf16[256,256]{1,0:T(8,128)(2,1)S(1)}, bf16[256,256]{1,0:T(8,128)(2,1)}, u32[]{:S(2)}) copy-start(bf16[256,256]{1,0:T(8,128)(2,1)} %param.19) | copy-start | bytes 393220
